TPU v7x, 128 devices: a whole 4x4x4 slice. The times are simulated.
128 devices in a mesh: seq: 16 (over z_hi, y, core), batch: 8 (over x, z_lo).
Axes of the slice: x: 4, y: 4, z: 4 (z_hi: 2, z_lo: 2; z = z_hi * 2 + z_lo), core: 2. Of those that a mesh axis runs over, the one named last changes fastest.
Arguments:
- tokens: bfloat16 [16, 1024, 1088], P('batch', 'seq'), may hold values from -6 to 6
- segments: int32 [16, 1024], P('batch', 'seq'), may hold values from 0 to 256, as said below
- adapter_pick: int32 [16], P('batch'), may hold values from 0 to 7
- norm_gain: float32 [2, 2, 1088], replicated, may hold values from 0.1 to 1.9
- w_qkv: bfloat16 [2, 3551232], P(None, ('seq', 'batch')), may hold values from -0.1875 to 0.1875
- w_out: bfloat16 [2, 1183744], P(None, ('seq', 'batch')), may hold values from -0.75 to 0.75
- w_up: bfloat16 [2, 4734976], P(None, ('seq', 'batch')), may hold values from -0.1875 to 0.1875
- w_down: bfloat16 [2, 4734976], P(None, ('seq', 'batch')), may hold values from -0.09375 to 0.09375
- a_qkv: bfloat16 [2, 1088, 128], replicated, may hold values from -0.1875 to 0.1875
- b_qkv: bfloat16 [2, 128, 3264], replicated, may hold values from -0.75 to 0.75
- a_out: bfloat16 [2, 1088, 128], replicated, may hold values from -0.1875 to 0.1875
- b_out: bfloat16 [2, 128, 1088], replicated, may hold values from -0.75 to 0.75
- a_up: bfloat16 [2, 1088, 128], replicated, may hold values from -0.1875 to 0.1875
- b_up: bfloat16 [2, 128, 4352], replicated, may hold values from -0.75 to 0.75
- a_down: bfloat16 [2, 4352, 128], replicated, may hold values from -0.09375 to 0.09375
- b_down: bfloat16 [2, 128, 1088], replicated, may hold values from -0.75 to 0.75
- grad_out: bfloat16 [16, 1024, 1088], P('batch', 'seq'), may hold values from -6 to 6
Outputs:
- out: bfloat16 [16, 1024, 1088], P('batch', 'seq')
- grad_tokens: float32 [16, 1024, 1088], P('batch', 'seq')
- grad_a_qkv: float32 [2, 1088, 128], replicated
- grad_b_qkv: float32 [2, 128, 3264], replicated
- grad_a_out: float32 [2, 1088, 128], replicated
- grad_b_out: float32 [2, 128, 1088], replicated
- grad_a_up: float32 [2, 1088, 128], replicated
- grad_b_up: float32 [2, 128, 4352], replicated
- grad_a_down: float32 [2, 4352, 128], replicated
- grad_b_down: float32 [2, 128, 1088], replicated
Inputs may be any that keep to these rules, and one draw needn't show every extreme that they name: `segments`: along each sequence the numbers start at 0 and rise by 0 or 1 from one position to the next; equal numbers mark one document. In one sequence of each group of 2 that share an index of batch, one document begins within the first 64 positions and ends within the last 64.
All inputs are finite; a program needn't handle non-finite values.
Results may differ from a plain program's by a relative error of at most 0.024.
Values may be sent and summed in bfloat16 or wider, within the bound.
No kernel may reach another device: no remote copies, remote signals or barrier semaphores. Data moves between devices by JAX's collectives and lax.ppermute only.
A program may use at most 320 MiB of HBM per device.

v0:
```python
import jax
import jax.numpy as jnp
from jax import lax
from jax.experimental import pallas as pl
from jax.experimental.pallas import tpu as pltpu
from jax.sharding import PartitionSpec as P

D = 1088
HEADS = 17
HEAD_DIM = 64
FF = 4352
RANK = 16
WIDE = 1152
PAIRS = 9
HALF = 64
KEYS = 1024
BF = jnp.bfloat16
F32 = jnp.float32
NEG = -1e30

SWAP = [(i, i ^ 8) for i in range(16)]
CORE = [(i, i ^ 1) for i in range(16)]
UP = [(i, (i & 8) | ((i + 2) & 7)) for i in range(16)]
DOWN = [(i, (i & 8) | ((i - 2) & 7)) for i in range(16)]
FAR = [(i, (i & 8) | ((i + 4) & 7)) for i in range(16)]
def at_chip(z, y, x, core):
    return ((z // 2 * 4 + y) * 2 + core) * 8 + x * 2 + z % 2


ALL = [[at_chip(z, y, x, c) for z in range(4) for y in range(4) for x in range(4) for c in range(2)]]
SAME_SEQUENCE = [[at_chip(z, y, x, c) for y in range(4) for c in range(2)] for z in range(4) for x in range(4)]
SAME_PLACE = [[at_chip(z, y, x, c) for z in range(4) for x in range(4)] for y in range(4) for c in range(2)]


def z_shift(by):
    return [
        (at_chip(z, y, x, c), at_chip((z + by) % 4, y, x, c))
        for z in range(4) for y in range(4) for x in range(4) for c in range(2)
    ]


def x_shift(by):
    return [(i, (i + 2 * by) % 8) for i in range(8)]


def y_shift(by):
    return [(i, (i & 8) | ((i + 2 * by) & 7)) for i in range(16)]


BOTH = ("seq", "batch")
SHIFTS = {"x": ("batch", x_shift), "y": ("seq", y_shift), "z": (BOTH, z_shift)}
TURNED = (D, D, D, FF, 3 * D, D, D)
PART_A, PART_B = 1664, 640
PART = PART_A + PART_B

LINES = 304
AT_OUT = 224
N_QKV, N_OUT, N_UP, N_DOWN = 217, 73, 289, 289
BLOCK = 136


def dot(a, b):
    return jnp.dot(a, b, preferred_element_type=F32)


def dot_t(a, b):
    return lax.dot_general(a, b, (((1,), (1,)), ((), ())), preferred_element_type=F32)


def t_dot(a, b):
    return lax.dot_general(a, b, (((0,), (0,)), ((), ())), preferred_element_type=F32)


def norm_stats(v):
    mean = jnp.mean(v, axis=-1, keepdims=True)
    centred = v - mean
    inv = lax.rsqrt(jnp.mean(centred * centred, axis=-1, keepdims=True) + 1e-05)
    return centred * inv, inv


def norm_back(v, gain, grad):
    r, inv = norm_stats(v)
    gr = grad * gain
    return inv * (
        gr - jnp.mean(gr, axis=-1, keepdims=True) - r * jnp.mean(gr * r, axis=-1, keepdims=True)
    )


def widen(a):
    return jnp.pad(a, ((0, 0), (0, WIDE - D)))


def lanes(rows):
    return lax.broadcasted_iota(jnp.int32, (rows, 128), 1)


def two_heads(block, single):
    low = lanes(block.shape[0]) < HEAD_DIM
    zero = jnp.zeros_like(block)
    first = jnp.where(low, block, zero)
    return first if single else jnp.concatenate([first, jnp.where(low, zero, block)], axis=0)


def one_block(stacked, single):
    rows = stacked.shape[0] if single else stacked.shape[0] // 2
    second = jnp.zeros_like(stacked) if single else stacked[rows:]
    return jnp.where(lanes(rows) < HEAD_DIM, stacked[:rows], second)


def pick_extra(rows, pair, single):
    spot = lanes(rows) - HEAD_DIM

    def of(h):
        return ((spot >= 3 * h) & (spot < 3 * h + 3)).astype(F32)

    head = 2 * pair
    return (of(head) if single else jnp.concatenate([of(head), of(head + 1)], axis=0)).astype(BF)


def heads_of_pair(pair):
    return 128 * pair, pair == PAIRS - 1


def gathered(own_ref, sib_ref, half, at):
    return jnp.concatenate(
        [ref[:, half, :, at : at + 128].reshape(4 * HALF, 128) for ref in (own_ref, sib_ref)], axis=0
    )


def row_terms(term):
    first = term.astype(BF).astype(F32)
    rest = term - first
    second = rest.astype(BF).astype(F32)
    third = rest - second
    turn = (lanes(term.shape[0]) - HEAD_DIM) % 3
    return jnp.where(turn == 0, first, jnp.where(turn == 1, second, third)).astype(BF)


def both(a, b):
    return jnp.concatenate([a, b], axis=0)


def fwd_kernel(q_ref, kv_own, kv_sib, lpos, lseg, kpos, kseg, ctx_ref, qe_ref):
    ok = (kpos[...] <= lpos[...]) & (kseg[...] == lseg[...])
    bias = jnp.where(ok, 0.0, NEG)
    bias = (both(bias[:HALF, : KEYS // 2], bias[:HALF, : KEYS // 2]), both(bias[HALF:], bias[HALF:]))
    spot = lanes(HALF) - HEAD_DIM
    terms = [jnp.zeros((HALF, 128), F32)] * 2
    for pair in range(PAIRS):
        at, single = heads_of_pair(pair)
        k_lo, k_hi = gathered(kv_own, kv_sib, 0, at), gathered(kv_own, kv_sib, 1, at)
        v_lo, v_hi = gathered(kv_own, kv_sib, 0, WIDE + at), gathered(kv_own, kv_sib, 1, WIDE + at)
        for half, keys, values in ((0, k_lo, v_lo), (1, both(k_lo, k_hi), both(v_lo, v_hi))):
            rows = two_heads(q_ref[half * HALF : (half + 1) * HALF, at : at + 128], single)
            s = dot_t(rows, keys) + bias[half][: rows.shape[0]]
            top = jnp.max(s, axis=1, keepdims=True)
            e = jnp.exp(s - top)
            total = jnp.sum(e, axis=1, keepdims=True)
            out = one_block(dot(e.astype(BF), values) * (1.0 / total), single)
            ctx_ref[half * HALF : (half + 1) * HALF, at : at + 128] = out.astype(BF)
            lse = top + jnp.log(total)
            for n in range(rows.shape[0] // HALF):
                head = 2 * pair + n
                mine = (spot >= 3 * head) & (spot < 3 * head + 3)
                terms[half] = jnp.where(mine, -lse[n * HALF : (n + 1) * HALF], terms[half])
    qe_ref[...] = q_ref[...]
    last = q_ref[:, WIDE - 128 :]
    qe_ref[:, WIDE - 128 :] = jnp.where(lanes(2 * HALF) < HEAD_DIM, last, row_terms(both(*terms)))


def dq_kernel(qe_ref, ge_ref, kv_own, kv_sib, lpos, lseg, kpos, kseg, gq_ref):
    ok = (kpos[...] <= lpos[...]) & (kseg[...] == lseg[...])
    bias = jnp.where(ok, 0.0, NEG)
    bias = (both(bias[:HALF, : KEYS // 2], bias[:HALF, : KEYS // 2]), both(bias[HALF:], bias[HALF:]))
    for pair in range(PAIRS):
        at, single = heads_of_pair(pair)
        k_lo, k_hi = gathered(kv_own, kv_sib, 0, at), gathered(kv_own, kv_sib, 1, at)
        v_lo, v_hi = gathered(kv_own, kv_sib, 0, WIDE + at), gathered(kv_own, kv_sib, 1, WIDE + at)
        mask = pick_extra(HALF, pair, single)
        for half, keys, values in ((0, k_lo, v_lo), (1, both(k_lo, k_hi), both(v_lo, v_hi))):
            place = slice(half * HALF, (half + 1) * HALF)
            ones = jnp.ones((keys.shape[0], 128), BF)

            def with_terms(ref):
                rows, extra = two_heads(ref[place, at : at + 128], single), ref[place, WIDE - 128 :]
                extra = extra if single else both(extra, extra)
                return jnp.concatenate([rows, extra * mask], axis=1)

            s = dot_t(with_terms(qe_ref), jnp.concatenate([keys, ones], axis=1))
            dp = dot_t(with_terms(ge_ref), jnp.concatenate([values, ones], axis=1))
            ds = (jnp.exp(s + bias[half][: s.shape[0]]) * dp).astype(BF)
            gq_ref[place, at : at + 128] = (one_block(dot(ds, keys), single) * 0.125).astype(BF)


def dkv_kernel(kv, q_own, q_sib, g_own, g_sib, lpos, lseg, kpos, kseg, gk_ref, gv_ref):
    ok = (lpos[...] <= kpos[...]) & (kseg[...] == lseg[...])
    bias = jnp.where(ok, 0.0, NEG)
    bias = (both(bias[:HALF], bias[:HALF]), both(bias[HALF:, KEYS // 2 :], bias[HALF:, KEYS // 2 :]))

    def queries(own, sib, at):
        lo, hi = gathered(own, sib, 0, at), gathered(own, sib, 1, at)
        return both(lo, hi), hi

    qx, gx = queries(q_own, q_sib, WIDE - 128), queries(g_own, g_sib, WIDE - 128)
    for pair in range(PAIRS):
        at, single = heads_of_pair(pair)
        q, g = queries(q_own, q_sib, at), queries(g_own, g_sib, at)
        terms = pick_extra(HALF, pair, single)
        for half in range(2):
            k = jnp.concatenate([two_heads(kv[half, :, at : at + 128], single), terms], axis=1)
            v = two_heads(kv[half, :, WIDE + at : WIDE + at + 128], single)
            v = jnp.concatenate([v, terms], axis=1)
            s = dot_t(k, jnp.concatenate([q[half], qx[half]], axis=1))
            p = jnp.exp(s + bias[half][: s.shape[0]])
            dp = dot_t(v, jnp.concatenate([g[half], gx[half]], axis=1))
            ds = (p * dp).astype(BF)
            gk_ref[half, :, at : at + 128] = one_block(dot(ds, q[half]), single).astype(BF)
            gv_ref[half, :, at : at + 128] = one_block(dot(p.astype(BF), g[half]), single).astype(BF)


ATTENTION_COST = pl.CostEstimate(
    flops=8_000_000_000, bytes_accessed=6 << 20, transcendentals=PAIRS * 256 * KEYS
)
PARAMS = pltpu.CompilerParams(vmem_limit_bytes=24 * 1024 * 1024)
HERE = pl.BlockSpec(memory_space=pltpu.VMEM)
ANYWHERE = pl.BlockSpec(memory_space=pl.ANY)
FLAT = jax.ShapeDtypeStruct((2 * HALF, WIDE), BF)


def attention_call(kernel, outs, *args):
    return pl.pallas_call(
        kernel,
        out_shape=outs,
        in_specs=[HERE] * len(args),
        out_specs=jax.tree.map(lambda _: HERE, outs),
        compiler_params=PARAMS,
        cost_estimate=ATTENTION_COST,
    )(*args)


def attend_fwd(q, kv_own, kv_sib, where):
    return attention_call(fwd_kernel, (FLAT, FLAT), q, kv_own, kv_sib, *where)


def attend_dq(qe, ge, kv_own, kv_sib, where):
    return attention_call(dq_kernel, FLAT, qe, ge, kv_own, kv_sib, *where)


def attend_dkv(kv, qe_own, qe_sib, ge_own, ge_sib, where):
    part = jax.ShapeDtypeStruct((2, HALF, WIDE), BF)
    return attention_call(dkv_kernel, (part, part), kv, qe_own, qe_sib, ge_own, ge_sib, *where)


FWD_PIECES = ((0, 1152), (1152, 2304), (2304, 3328), (3328, FF))
BACK_PIECES = ((0, FF // 2), (FF // 2, FF))
ROWS = 2 * HALF


def normalised(v):
    mean = jnp.mean(v, axis=1, keepdims=True)
    centred = v - mean
    inv = lax.rsqrt(jnp.mean(centred * centred, axis=1, keepdims=True) + 1e-05)
    return centred * inv, inv


def weight_copies(pieces, wout, wup, wdown, wout_here, wup_here, wdown_here, sems):
    out = pltpu.make_async_copy(wout, wout_here, sems.at[0])
    ups, downs = [], []
    for k, (a, b) in enumerate(pieces):
        ups.append(pltpu.make_async_copy(wup.at[:, a:b], wup_here.at[:, a:b], sems.at[1 + 2 * k]))
        downs.append(pltpu.make_async_copy(wdown.at[a:b, :], wdown_here.at[a:b, :], sems.at[2 + 2 * k]))
    return out, ups, downs


def mlp_fwd_kernel(
    ctx, hidden, gain, gain_next, a_o, b_o, a_u, b_d, b_u, a_d, wout, wup, wdown,
    middle, n2, low_o, low_u, low_d, after, n1_next, wout_here, wup_here, wdown_here, sems
):
    out, ups, downs = weight_copies(FWD_PIECES, wout, wup, wdown, wout_here, wup_here, wdown_here, sems)
    out.start()
    for up, down in zip(ups, downs):
        up.start()
        down.start()
    x = ctx[:, :D]
    low = dot(x, a_o[...]).astype(BF)
    low_o[...] = low
    out.wait()
    mid = hidden[...] + dot(x, wout_here[...]) + dot(low, b_o[...])
    middle[...] = mid
    normed = (normalised(mid)[0] * gain[...]).astype(BF)
    n2[...] = normed
    low = dot(normed, a_u[...]).astype(BF)
    low_u[...] = low
    total, total_low = jnp.zeros((ROWS, D), F32), jnp.zeros((ROWS, RANK), F32)
    for k, (a, b) in enumerate(FWD_PIECES):
        ups[k].wait()
        up = dot(normed, wup_here[:, a:b]) + dot(low, b_u[:, a:b])
        act = (up * (0.5 * (1.0 + lax.erf(up * 0.7071067811865476)))).astype(BF)
        downs[k].wait()
        total = total + dot(act, wdown_here[a:b, :])
        total_low = total_low + dot(act, a_d[a:b, :])
    low = total_low.astype(BF)
    low_d[...] = low
    new = middle[...] + (total + dot(low, b_d[...]))
    after[...] = new
    n1_next[...] = (normalised(new)[0] * gain_next[...]).astype(BF)


def mlp_back_kernel(
    g, ctx, middle, gain, n2, low_o, low_u, low_d, a_o, b_o, a_u, b_d, spread, b_u, a_d, wout, wup, wdown,
    gh2, ge, ga_o, gb_o, ga_u, gb_d, ga_d, gb_u, wout_here, wup_here, wdown_here, sems
):
    out, ups, downs = weight_copies(BACK_PIECES, wout, wup, wdown, wout_here, wup_here, wdown_here, sems)
    for up, down in zip(ups, downs):
        up.start()
        down.start()
    out.start()
    gy = g[...].astype(BF)
    glow_d = dot_t(gy, b_d[...]).astype(BF)
    gb_d[...] = t_dot(low_d[...], gy).astype(BF)
    normed, low = n2[...], low_u[...]
    gn2, glow_u = jnp.zeros((ROWS, D), F32), jnp.zeros((ROWS, RANK), F32)
    for k, (a, b) in enumerate(BACK_PIECES):
        ups[k].wait()
        up = dot(normed, wup_here[:, a:b]) + dot(low, b_u[:, a:b])
        phi = 0.5 * (1.0 + lax.erf(up * 0.7071067811865476))
        ga_d[:, a:b] = t_dot(glow_d, (up * phi).astype(BF)).astype(BF)
        downs[k].wait()
        gact = dot_t(gy, wdown_here[a:b, :]) + dot_t(glow_d, a_d[a:b, :])
        density = jnp.exp(-0.5 * up * up) * 0.3989422804014327
        gup = (gact * (phi + up * density)).astype(BF)
        gb_u[:, a:b] = t_dot(low, gup).astype(BF)
        gn2 = gn2 + dot_t(gup, wup_here[:, a:b])
        glow_u = glow_u + dot_t(gup, b_u[:, a:b])
    glow_u = glow_u.astype(BF)
    gn2 = gn2 + dot_t(glow_u, a_u[...])
    ga_u[...] = t_dot(glow_u, normed).astype(BF)
    out.wait()
    through_norm(g, middle[...], gain, gn2, ctx[:, :D], low_o[...], a_o, b_o, wout_here, spread, gh2, ge, ga_o, gb_o)


def through_norm(g, middle, gain, gn2, x, low_o, a_o, b_o, wout, spread, gh2, ge, ga_o, gb_o):
    r, inv = normalised(middle)
    gr = gn2 * gain[...]
    grad = g[...] + inv * (
        gr - jnp.mean(gr, axis=1, keepdims=True) - r * jnp.mean(gr * r, axis=1, keepdims=True)
    )
    gh2[...] = grad
    gproj = grad.astype(BF)
    glow_o = dot_t(gproj, b_o[...]).astype(BF)
    ga_o[...] = t_dot(glow_o, x).astype(BF)
    gb_o[...] = t_dot(low_o, gproj).astype(BF)
    gctx = (dot_t(gproj, wout[...]) + dot_t(glow_o, a_o[...])).astype(BF)
    product = gctx.astype(F32) * x.astype(F32)
    first = product.astype(BF)
    second = (product - first.astype(F32)).astype(BF)
    delta = dot(first, spread[...]) + dot(second, spread[...])
    ge[:, :D] = gctx
    ge[:, D:] = row_terms(-delta)[:, HEAD_DIM:]


def qkv_back_kernel(
    gq, gk, gv, low, n1, a, b_q, b_kv, hidden, gain, gh2, wq, wkv, g, ga, gb_q, gb_kv, wq_here, wkv_here, sems
):
    first = pltpu.make_async_copy(wq, wq_here, sems.at[0])
    second = pltpu.make_async_copy(wkv, wkv_here, sems.at[1])
    first.start()
    second.start()
    q, k, v = gq[...], gk[...].reshape(ROWS, WIDE), gv[...].reshape(ROWS, WIDE)
    glow = dot_t(q, b_q[...]) + dot_t(k, b_kv[:, :WIDE]) + dot_t(v, b_kv[:, WIDE:])
    glow = glow.astype(BF)
    ga[...] = t_dot(glow, n1[...]).astype(BF)
    gb_q[...] = t_dot(low[...], q).astype(BF)
    gb_kv[:, :WIDE] = t_dot(low[...], k).astype(BF)
    gb_kv[:, WIDE:] = t_dot(low[...], v).astype(BF)
    first.wait()
    gn1 = dot_t(q, wq_here[...])
    second.wait()
    gn1 = gn1 + dot_t(k, wkv_here[:, :WIDE]) + dot_t(v, wkv_here[:, WIDE:]) + dot_t(glow, a[...])
    r, inv = normalised(hidden[...])
    gr = gn1 * gain[...]
    g[...] = gh2[...] + inv * (
        gr - jnp.mean(gr, axis=1, keepdims=True) - r * jnp.mean(gr * r, axis=1, keepdims=True)
    )


def mlp_both_kernel(
    ctx, hidden, gain, g, a_o, b_o, a_u, b_d, spread, b_u, a_d, wout, wup, wdown,
    after, gh2, ge, ga_o, gb_o, ga_u, gb_d, ga_d, gb_u, wout_here, wup_here, wdown_here, sems
):
    out, ups, downs = weight_copies(BACK_PIECES, wout, wup, wdown, wout_here, wup_here, wdown_here, sems)
    out.start()
    for up, down in zip(ups, downs):
        up.start()
        down.start()
    x = ctx[:, :D]
    low_o = dot(x, a_o[...]).astype(BF)
    out.wait()
    gh2[...] = hidden[...] + dot(x, wout_here[...]) + dot(low_o, b_o[...])
    normed = (normalised(gh2[...])[0] * gain[...]).astype(BF)
    low = dot(normed, a_u[...]).astype(BF)
    gy = g[...].astype(BF)
    glow_d = dot_t(gy, b_d[...]).astype(BF)
    total, total_low = jnp.zeros((ROWS, D), F32), jnp.zeros((ROWS, RANK), F32)
    gn2, glow_u = jnp.zeros((ROWS, D), F32), jnp.zeros((ROWS, RANK), F32)
    for k, (a, b) in enumerate(BACK_PIECES):
        ups[k].wait()
        up = dot(normed, wup_here[:, a:b]) + dot(low, b_u[:, a:b])
        phi = 0.5 * (1.0 + lax.erf(up * 0.7071067811865476))
        act = (up * phi).astype(BF)
        ga_d[:, a:b] = t_dot(glow_d, act).astype(BF)
        downs[k].wait()
        total = total + dot(act, wdown_here[a:b, :])
        total_low = total_low + dot(act, a_d[a:b, :])
        gact = dot_t(gy, wdown_here[a:b, :]) + dot_t(glow_d, a_d[a:b, :])
        density = jnp.exp(-0.5 * up * up) * 0.3989422804014327
        gup = (gact * (phi + up * density)).astype(BF)
        gb_u[:, a:b] = t_dot(low, gup).astype(BF)
        gn2 = gn2 + dot_t(gup, wup_here[:, a:b])
        glow_u = glow_u + dot_t(gup, b_u[:, a:b])
    low_d = total_low.astype(BF)
    gb_d[...] = t_dot(low_d, gy).astype(BF)
    after[...] = (gh2[...] + (total + dot(low_d, b_d[...]))).astype(BF)
    glow_u = glow_u.astype(BF)
    gn2 = gn2 + dot_t(glow_u, a_u[...])
    ga_u[...] = t_dot(glow_u, normed).astype(BF)
    through_norm(g, gh2[...], gain, gn2, x, low_o, a_o, b_o, wout_here, spread, gh2, ge, ga_o, gb_o)


def shape_of(rows, width, kind=BF):
    return jax.ShapeDtypeStruct((rows, width), kind)


def mlp_call(kernel, pieces, args, outs, flops, limit=40):
    return pl.pallas_call(
        kernel,
        out_shape=outs,
        in_specs=[HERE] * (len(args) - 3) + [ANYWHERE] * 3,
        out_specs=(HERE,) * len(outs),
        scratch_shapes=[
            pltpu.VMEM((D, D), BF),
            pltpu.VMEM((D, FF), BF),
            pltpu.VMEM((FF, D), BF),
            pltpu.SemaphoreType.DMA((1 + 2 * len(pieces),)),
        ],
        compiler_params=pltpu.CompilerParams(vmem_limit_bytes=limit * 1024 * 1024),
        cost_estimate=pl.CostEstimate(flops=flops, bytes_accessed=24 << 20, transcendentals=ROWS * FF),
    )(*args)


def mlp_fwd(*args):
    outs = (shape_of(ROWS, D, F32), shape_of(ROWS, D)) + (shape_of(ROWS, RANK),) * 3
    outs += (shape_of(ROWS, D, F32), shape_of(ROWS, D))
    return mlp_call(mlp_fwd_kernel, FWD_PIECES, args, outs, 10_000_000_000)


def mlp_both(*args):
    outs = (shape_of(ROWS, D), shape_of(ROWS, D, F32), shape_of(ROWS, WIDE)) + (shape_of(RANK, D),) * 4
    outs += (shape_of(RANK, FF),) * 2
    return mlp_call(mlp_both_kernel, BACK_PIECES, args, outs, 18_000_000_000)


def qkv_back(*args):
    return pl.pallas_call(
        qkv_back_kernel,
        out_shape=(shape_of(ROWS, D, F32), shape_of(RANK, D), shape_of(RANK, WIDE), shape_of(RANK, 2 * WIDE)),
        in_specs=[HERE] * 11 + [ANYWHERE] * 2,
        out_specs=(HERE,) * 4,
        scratch_shapes=[
            pltpu.VMEM((D, WIDE), BF),
            pltpu.VMEM((D, 2 * WIDE), BF),
            pltpu.SemaphoreType.DMA((2,)),
        ],
        compiler_params=pltpu.CompilerParams(vmem_limit_bytes=20 * 1024 * 1024),
        cost_estimate=pl.CostEstimate(flops=5_000_000_000, bytes_accessed=10 << 20, transcendentals=0),
    )(*args)


def mlp_back(*args):
    outs = (shape_of(ROWS, D, F32), shape_of(ROWS, WIDE)) + (shape_of(RANK, D),) * 4
    outs += (shape_of(RANK, FF),) * 2
    return mlp_call(mlp_back_kernel, BACK_PIECES, args, outs, 16_000_000_000, 56)


def ring_start(block):
    return lax.ppermute(block, "seq", UP), lax.ppermute(block, "seq", DOWN)


def ring_far(block, before, after):
    far_lo = lax.ppermute(before[0], "seq", UP)
    far_hi = lax.ppermute(after[1], "seq", DOWN)
    return jnp.stack([block, before, after, jnp.stack([far_lo, far_hi])])


def other_core(own):
    return lax.ppermute(own, "seq", CORE)


def sum_sequence(parts, core, y):
    parts = parts.reshape((4, 2) + parts.shape[1:])
    mine = lax.dynamic_index_in_dim(parts, core, 1, keepdims=False)
    other = lax.dynamic_index_in_dim(parts, 1 - core, 1, keepdims=False)
    half = mine.astype(F32) + lax.ppermute(other, "seq", CORE).astype(F32)

    def of(step):
        return lax.dynamic_index_in_dim(half, (y + step) % 4, 0, keepdims=False)

    total = of(0)
    for step, route in ((1, UP), (3, DOWN), (2, FAR)):
        total = total + lax.ppermute(of(step).astype(BF), "seq", route).astype(F32)
    return total


def tie(*values):
    return lax.optimization_barrier(values)


def eighths(turned, straight):
    def cut(a, part):
        return jnp.pad(a, ((0, 0), (0, 8 * part - a.shape[1]))).reshape(RANK, 8, part)

    first = cut(jnp.concatenate(turned, axis=1), PART_A)
    return jnp.swapaxes(jnp.concatenate([first, cut(straight, PART_B)], axis=2), 0, 1)


def by_adapter_kernel(picks, *refs):
    parts, out_ref, acc = refs[:-2], refs[-2], refs[-1]
    acc[...] = jnp.zeros_like(acc)
    at = 0
    for ref in parts:
        for k in range(ref.shape[0]):
            rows = pl.ds(pl.multiple_of(picks[at] * RANK, RANK), RANK)
            acc[rows, :] = acc[rows, :] + ref[k].astype(F32)
            at += 1
    for j in range(PART // 128):
        square = acc[:, 128 * j : 128 * (j + 1)]
        square = square.T if 128 * j < PART_A else square
        out_ref[128 * j : 128 * (j + 1), :] = square.astype(BF)


def by_adapter(parts, picks):
    return pl.pallas_call(
        by_adapter_kernel,
        out_shape=jax.ShapeDtypeStruct((PART, 128), BF),
        in_specs=[pl.BlockSpec(memory_space=pltpu.SMEM)]
        + [pl.BlockSpec(memory_space=pltpu.VMEM)] * len(parts),
        out_specs=pl.BlockSpec(memory_space=pltpu.VMEM),
        scratch_shapes=[pltpu.VMEM((8 * RANK, PART), F32)],
        compiler_params=PARAMS,
        cost_estimate=pl.CostEstimate(flops=16 * RANK * PART, bytes_accessed=2 << 20, transcendentals=0),
    )(picks, *parts)


def unfold_rows(layer, rows, outs):
    turned, straight = outs[:-1], outs[-1]
    start = 0
    for out, width in zip(turned, TURNED):
        at = start
        while at < start + width:
            n = min(start + width, (at // PART_A + 1) * PART_A) - at
            out[layer, at - start : at - start + n, :] = rows(at // PART_A, at % PART_A, n)
            at += n
        start += width
    squares = PART_B // 128
    for t in range(FF // 128):
        value = rows(t // squares, PART_A + 128 * (t % squares), 128)
        straight[layer, :, 128 * t : 128 * (t + 1)] = value


def unfold_late_kernel(ref, *outs):
    unfold_rows(0, lambda e, at, n: ref[e, at : at + n, :].astype(F32), outs)


def unfold_kernel(place, own_ref, sib_ref, *refs):
    half = len(refs) // 2

    def rows(e, at, n):
        k = place[e]
        mine = own_ref[k % 4, at : at + n, :]
        other = sib_ref[k % 4, at : at + n, :]
        return jnp.where(k < 4, mine.astype(F32), other.astype(F32))

    unfold_rows(0, rows, refs[half:])


def one_layer(layer, *shape):
    return pl.BlockSpec((1,) + shape, lambda i: (layer, 0, 0))


def unfold(kernel, layer, *args):
    shapes = [(w, 128) for w in TURNED] + [(128, FF)]
    whole = [jax.ShapeDtypeStruct((2,) + shape, F32) for shape in shapes]
    first, earlier = (args, ()) if layer == 1 else (args[:3], args[3])
    specs = [pl.BlockSpec(memory_space=pltpu.SMEM)] if layer == 0 else []
    specs += [fixed(*a.shape) for a in first[len(specs) :]] + [ANYWHERE] * len(earlier)
    return pl.pallas_call(
        kernel,
        grid=(1,),
        out_shape=tuple(whole),
        in_specs=specs,
        out_specs=tuple(one_layer(layer, *shape) for shape in shapes),
        input_output_aliases={3 + n: n for n in range(len(earlier))},
        compiler_params=pltpu.CompilerParams(vmem_limit_bytes=40 * 1024 * 1024),
        cost_estimate=pl.CostEstimate(flops=0, bytes_accessed=14 << 20, transcendentals=0),
    )(*first, *earlier)


def fixed(*shape):
    return pl.BlockSpec(shape, lambda i: (0,) * len(shape))


def share(w_qkv, w_out, w_up, w_down, z_lo, spare):
    def half_row(w, front, lines):
        size = lines * 128 - w.shape[1]
        first = jnp.pad(w, ((0, 0), (0, size)))
        second = jnp.pad(w, ((0, 0), (front, size - front)))
        return jnp.where(z_lo == 0, first, second).reshape(-1, lines, 128)

    def put(a, room):
        return jnp.pad(a, ((0, 0), (0, room - a.shape[1]), (0, 0)))

    extra = jnp.broadcast_to(spare[None], (2, 1, 128))
    attention = [
        put(half_row(w_qkv, 32, N_QKV), AT_OUT),
        put(half_row(w_out, 32, N_OUT), LINES - AT_OUT - 1),
        extra,
    ]
    up, down = put(w_up.reshape(-1, N_UP, 128), LINES), put(w_down.reshape(-1, N_DOWN, 128), LINES - 1)
    return jnp.concatenate(attention, axis=1), jnp.concatenate([up, down, extra], axis=1)


def spin(a):
    return pltpu.roll(a, HEAD_DIM, 1)


def fill(ref, base, lines):
    ref[pl.ds(base, lines.shape[0], stride=2), :] = lines


def between(ref, base, n):
    now, later = ref[pl.ds(base, n, stride=2), :], ref[pl.ds(base + 2, n, stride=2), :]
    ref[pl.ds(base + 1, n, stride=2), :] = spin(jnp.where(lanes(n) < HEAD_DIM, later, now))


def columns(ref, dst, to, start, units, step=2):
    got = ref[pl.ds(start, dst.shape[0], stride=units), :].astype(BF)
    n = min(128, dst.shape[1] - to)
    dst[:, to : to + n] = got[:, :n]


def lines_of(ref, pair, zl, start, n):
    return ref[0, zl, 0, pair % 4, pair // 4, start : start + n, :].astype(F32)


def unpack_attention_kernel(g_ref, *refs):
    def lines(pair, zl):
        return lines_of(g_ref, pair, zl, 0, N_QKV), lines_of(g_ref, pair, zl, AT_OUT, N_OUT)

    unpack_attention_lines(lines, *refs)


def unpack_first_kernel(steps, own_1, sib_1, own_2, sib_2, *refs):
    def lines(pair, zl):
        x, core = pair % 4, pair // 4
        z_at, x_at = steps[4 + 2 * (pl.program_id(0) // 4) + zl], steps[8 + x]
        mine = steps[12] == core
        top = jnp.where(mine, own_1[z_at, 0, x_at], sib_1[z_at, 0, x_at])
        bottom = jnp.where(mine, own_2[0, z_at, x_at], sib_2[0, z_at, x_at])
        both = jnp.concatenate([top.astype(F32), bottom.astype(F32)], axis=0)
        return both[:N_QKV], both[AT_OUT : AT_OUT + N_OUT]

    unpack_attention_lines(lines, *refs)


def unpack_attention_lines(lines, q_ref, kv_ref, out_ref, s_qkv, s_out):
    low = lanes(1) < HEAD_DIM
    zero = jnp.zeros((1, 128), F32)
    for pair in range(8):
        (qkv0, out0), (qkv1, out1) = lines(pair, 0), lines(pair, 1)
        base, base_out = pair * 867, pair * 289
        fill(s_qkv, base, qkv0)
        fill(s_qkv, base + 433, qkv1)
        between(s_qkv, base, N_QKV - 1)
        between(s_qkv, base + 433, N_QKV)
        s_qkv[pl.ds(base + 432, 1), :] = qkv0[N_QKV - 1 :] + spin(jnp.where(low, qkv1[:1], zero))
        s_qkv[pl.ds(base + 433, 1), :] = qkv1[:1] + spin(jnp.where(low, zero, qkv0[N_QKV - 1 :]))
        fill(s_out, base_out, out0)
        fill(s_out, base_out + 144, out1)
        s_out[pl.ds(base_out + 144, 1), :] = out0[N_OUT - 1 :] + out1[:1]
        between(s_out, base_out, N_OUT - 1)
        between(s_out, base_out + 144, N_OUT - 1)
    half = lanes(BLOCK) < HEAD_DIM
    for dst, to, first in ((q_ref, 0, 0), (kv_ref, 0, 17), (kv_ref, WIDE, 34)):
        for j in range(8):
            columns(s_qkv, dst, to + 128 * j, first + 2 * j, 51)
        got = s_qkv[pl.ds(first + 16, BLOCK, stride=51), :]
        dst[:, to + D - HEAD_DIM : to + WIDE] = jnp.where(half, got, 0.0).astype(BF)
    for j in range(9):
        columns(s_out, out_ref, 128 * j, 2 * j, 17)


def unpack_mlp_kernel(g_up, g_down, up_ref, down_ref, s_up, s_down):
    for pair in range(8):
        for zl in range(2):
            at = pair * 2 + zl
            s_up[pl.ds(at * N_UP, N_UP), :] = lines_of(g_up, pair, zl, 0, N_UP)
            fill(s_down, at * 2 * N_DOWN, lines_of(g_down, pair, zl, 0, N_DOWN))
    for at in range(16):
        between(s_down, at * 2 * N_DOWN, N_DOWN)
    for j in range(34):
        columns(s_up, up_ref, 128 * j, j, 34)
    for j in range(9):
        columns(s_down, down_ref, 128 * j, 2 * j, 17)


def unpack(kernel, got, at, outs, scratch_lines):
    g = got.reshape(2, 2, 4, 4, 2, -1, 128)

    def spec(k):
        return pl.BlockSpec((1, 2, 1, 4, 2, LINES, 128), lambda i: (i // 4, 0, i % 4, 0, 0, k, 0))

    return pl.pallas_call(
        kernel,
        grid=(8,),
        out_shape=tuple(jax.ShapeDtypeStruct((8 * r, w), BF) for r, w in outs),
        in_specs=[spec(k) for k in at],
        out_specs=tuple(pl.BlockSpec((r, w), lambda i: (i, 0)) for r, w in outs),
        scratch_shapes=[pltpu.VMEM((n, 128), F32) for n in scratch_lines],
        compiler_params=pltpu.CompilerParams(vmem_limit_bytes=26 * 1024 * 1024),
        cost_estimate=pl.CostEstimate(
            flops=0, bytes_accessed=len(at) * (20 << 20), transcendentals=0
        ),
    )(*[g] * len(at))


ATTENTION_OUTS = [(BLOCK, WIDE), (BLOCK, 2 * WIDE), (BLOCK, D)]
ATTENTION_LINES = [8 * 867 + 8, 8 * 289 + 8]


def unpack_attention(got, at):
    return unpack(unpack_attention_kernel, got, [at], ATTENTION_OUTS, ATTENTION_LINES)


def along(axis, block, near):
    name, shift = SHIFTS[axis]
    before = lax.ppermute(block, name, shift(1))
    after = lax.ppermute(block, name, shift(-1))
    if near:
        far = lax.ppermute(block, name, shift(2))
    else:
        n = block.shape[0] // 2
        far = [lax.ppermute(before[:n], name, shift(1)), lax.ppermute(after[n:], name, shift(-1))]
        far = jnp.concatenate(far)
    return jnp.stack([block, before, after, far])


def gather_first(share, later):
    n = LINES // 2
    row = along("x", share, True)
    one, two = along("y", row[:, :n], True), along("z", row[:, n:], True)
    one, two, later = tie(one, two, later)
    one, two = along("z", one, False), along("y", two, False)
    return (one, other_core(one), two, other_core(two)), later


def unpack_first(one, sib_one, two, sib_two, steps):
    n = LINES // 2
    spec_one = pl.BlockSpec((4, 1, 4, n, 128), lambda i, steps: (0, steps[i % 4], 0, 0, 0))
    spec_two = pl.BlockSpec((1, 4, 4, n, 128), lambda i, steps: (steps[i % 4], 0, 0, 0, 0))
    return pl.pallas_call(
        unpack_first_kernel,
        grid_spec=pltpu.PrefetchScalarGridSpec(
            num_scalar_prefetch=1,
            grid=(8,),
            in_specs=[spec_one, spec_one, spec_two, spec_two],
            out_specs=tuple(pl.BlockSpec((r, w), lambda i, steps: (i, 0)) for r, w in ATTENTION_OUTS),
            scratch_shapes=[pltpu.VMEM((n, 128), F32) for n in ATTENTION_LINES],
        ),
        out_shape=tuple(jax.ShapeDtypeStruct((8 * r, w), BF) for r, w in ATTENTION_OUTS),
        compiler_params=pltpu.CompilerParams(vmem_limit_bytes=26 * 1024 * 1024),
        cost_estimate=pl.CostEstimate(flops=0, bytes_accessed=30 << 20, transcendentals=0),
    )(steps, one, sib_one, two, sib_two)


def unpack_mlp(got, at):
    outs = [(BLOCK, FF), (4 * BLOCK, D)]
    return unpack(unpack_mlp_kernel, got, [at, at + 1], outs, [16 * N_UP, 32 * N_DOWN + 8])


def shards(
    tokens, segments, adapter_pick, norm_gain, w_qkv, w_out, w_up, w_down,
    a_qkv, b_qkv, a_out, b_out, a_up, b_up, a_down, b_down, grad_out
):
    layers = norm_gain.shape[0]
    index = lax.axis_index("seq")
    z_hi, place = index // 8, index % 8
    core, y = place % 2, place // 2

    def halves(own, other):
        return jnp.where(z_hi == 0, jnp.stack([own, other]), jnp.stack([other, own]))

    def mine(a):
        return lax.dynamic_index_in_dim(a, z_hi, 0, keepdims=False)

    def theirs(a):
        return lax.dynamic_index_in_dim(a, 1 - z_hi, 0, keepdims=False)

    batch = lax.axis_index("batch")
    spare = (segments.reshape(1, 128), jnp.pad(adapter_pick[None], ((0, 0), (0, 126))))
    attention, _ = share(w_qkv, w_out, w_up, w_down, batch % 2, spare[0].astype(BF))
    _, mlp = share(w_qkv, w_out, w_up, w_down, batch % 2, spare[1].astype(BF))

    def gather(a):
        return lax.all_gather(a, BOTH, axis=0, tiled=True, axis_index_groups=ALL)

    early = gather(jnp.concatenate([mlp[0], attention[1]], axis=0))
    late = gather(mlp[1])
    raw = (a_qkv, b_qkv, a_out, b_out, a_up, b_up, a_down, b_down, norm_gain)
    (one, sib_one, two, sib_two), raw = gather_first(attention[0], raw)
    a_qkv, b_qkv, a_out, b_out, a_up, b_up, a_down, b_down, norm_gain = raw

    sent = lax.ppermute(jnp.stack([theirs(tokens), theirs(grad_out)]), "seq", SWAP)
    hidden = halves(mine(tokens), sent[0]).reshape(2 * HALF, D).astype(F32)
    grad_hidden = halves(mine(grad_out), sent[1]).reshape(2 * HALF, D).astype(F32)
    pick = mine(adapter_pick)

    def segments_of(two):
        lines = two[:, :, 0, -1]
        lines = jnp.stack([lines[:, 0], lines[:, 3]])
        return lax.dynamic_slice(lines, (0, 0, z_hi * HALF), (2, 4, HALF))

    seg = jnp.stack([segments_of(two), segments_of(sib_two)], axis=1)
    seg = jnp.where(z_hi == 0, seg, seg[::-1]).astype(jnp.int32)
    offset = jnp.arange(HALF, dtype=jnp.int32)
    start = jnp.array([0, KEYS // 2], jnp.int32)[:, None]
    lpos = (start + place * HALF + offset[None]).reshape(2 * HALF, 1)
    lseg = seg[:, 0, 0].reshape(2 * HALF, 1)
    ys = (y + jnp.array([0, 3, 1, 2], jnp.int32)) % 4
    order = jnp.concatenate([2 * ys + core, 2 * ys + 1 - core])
    kpos = (start[:, :, None] + (order * HALF)[None, :, None] + offset).reshape(1, KEYS)
    where = (lpos, lseg, kpos, seg.reshape(1, KEYS))

    z_lo, x = batch % 2, batch // 2
    z = z_hi * 2 + z_lo
    picks = early.reshape(2, 2, 4, 4, 2, -1, 128)[0, :, 0, :, 0, 2 * LINES - 1, :2].astype(jnp.int32)
    picks = jnp.swapaxes(picks, 0, 1).reshape(16)
    steps = jnp.array([0, 3, 1, 2], jnp.int32)

    def sequence(zs, xs):
        return 2 * (2 * xs + zs % 2) + zs // 2

    four = jnp.arange(4, dtype=jnp.int32)
    picks_in_order = jnp.take(picks, sequence(four[:, None], four[None, :]).reshape(16))
    zs, xs = (z + steps) % 4, (x + steps) % 4
    picks_by_step = jnp.take(picks, sequence(zs[None, :], xs[:, None]).reshape(16))
    eight = jnp.arange(8, dtype=jnp.int32)
    back = jnp.array([0, 2, 3, 1], jnp.int32)
    place_by_step = 4 * ((eight % 2) ^ core) + jnp.take(back, (eight // 2 - y) % 4)
    arrival = [jnp.take(back, (four - at) % 4) for at in (y, z, x)]
    arrival = jnp.concatenate(arrival + [core[None]]).astype(jnp.int32)

    def low_in(a, l):
        return lax.dynamic_slice_in_dim(a[l], pick * RANK, RANK, 1)

    def low_out(b, l):
        return lax.dynamic_slice_in_dim(b[l], pick * RANK, RANK, 0)

    heads_of = (jnp.arange(D, dtype=jnp.int32) // HEAD_DIM)[:, None]
    spread = (heads_of == (jnp.arange(128, dtype=jnp.int32)[None, :] - HEAD_DIM) // 3).astype(BF)

    def adapters(l):
        b_first = low_out(b_qkv, l)
        b_kv = jnp.concatenate([widen(b_first[:, D : 2 * D]), widen(b_first[:, 2 * D :])], axis=1)
        rest = [f(a, l) for pair in ((a_out, b_out), (a_up, b_up), (a_down, b_down)) for f, a in zip((low_in, low_out), pair)]
        return [low_in(a_qkv, l), widen(b_first[:, :D]), b_kv] + rest

    n1 = (norm_stats(hidden)[0] * norm_gain[0, 0]).astype(BF)
    ahead = (where, spread, n1, grad_hidden, [adapters(l) for l in range(layers)])
    sib_one, (where, spread, n1, grad_hidden, adapter_parts) = tie(sib_one, ahead)
    first = unpack_first(one, sib_one, two, sib_two, arrival)
    saved, queries = [], []
    for l in range(layers):
        a_first, b_q, b_kv, a_o, b_o, a_u, b_u, a_d, b_d = adapter_parts[l]
        wq, wkv, wout = first
        low_qkv = dot(n1, a_first).astype(BF)
        kv = (dot(n1, wkv) + dot(low_qkv, b_kv)).astype(BF).reshape(2, HALF, 2 * WIDE)
        q = (dot(n1, wq) + dot(low_qkv, b_q)).astype(BF) * jnp.asarray(0.125, BF)
        before, after = ring_start(kv)
        if l == 0:
            wup, wdown = unpack_mlp(early, 0)
            before, after, q, wup, wdown = tie(before, after, q, wup, wdown)
        else:
            before, after, q, qe_own = tie(before, after, q, qe_own)
            queries.append((qe_own, other_core(qe_own)))
        kv_own = ring_far(kv, before, after)
        if l > 0:
            late, kv_own = tie(late, kv_own)
            wup, wdown = unpack_mlp(late, 0)
        if l == 0:
            first = unpack_attention(early, 2)
            kv_own, *first = tie(kv_own, *first)
        kv_sib = other_core(kv_own)
        ctx, qe = attend_fwd(q, kv_own, kv_sib, where)
        qe = qe.reshape(2, HALF, WIDE)
        q_before, q_after = ring_start(qe)
        gains = norm_gain[l, 1][None], norm_gain[(l + 1) % layers, 0][None]
        small, large = (a_o, b_o, a_u, b_d), (b_u, a_d, wout, wup, wdown)
        rows, hidden_next, n1_next = None, None, None
        if l < layers - 1:
            middle, n2, low_o, low_u, low_d, hidden_next, n1_next = mlp_fwd(ctx, hidden, *gains, *small, *large)
            q_before, q_after, hidden_next, n1_next = tie(q_before, q_after, hidden_next, n1_next)
            rows = (ctx, middle, gains[0], n2, low_o, low_u, low_d)
        else:
            result, *back = mlp_both(ctx, hidden, gains[0], grad_hidden, *small, spread, *large)
            q_before, q_after, *back = tie(q_before, q_after, *back)
        qe_own = ring_far(qe, q_before, q_after)
        saved.append(
            (hidden, n1, low_qkv, kv, kv_own, kv_sib, qe.reshape(2 * HALF, WIDE))
            + (rows, small, large, a_first, b_q, b_kv, wq, wkv)
        )
        hidden, n1 = hidden_next, n1_next

    behind = None
    for l in reversed(range(layers)):
        hidden_in, n1, low_qkv, kv, kv_own, kv_sib, qe, rows, small, large, a_first, b_q, b_kv, wq, wkv = saved[l]
        if l < layers - 1:
            back = mlp_back(g, *rows, *small, spread, *large)
        gh2, ge, ga_o, gb_o, ga_u, gb_d, ga_d, gb_u = back
        if l == layers - 1:
            qe_own, ge = tie(qe_own, ge)
            qe_sib = other_core(qe_own)
        else:
            qe_own, qe_sib = queries[l]
        g_block = ge.reshape(2, HALF, WIDE)
        g_before, g_after = ring_start(g_block)
        if behind is not None:
            behind, ge = tie(behind, ge)
            behind = lax.all_gather(behind, BOTH, axis=0, axis_index_groups=SAME_PLACE)
        gq = attend_dq(qe, ge, kv_own, kv_sib, where)
        g_before, g_after, gq = tie(g_before, g_after, gq)
        ge_own = ring_far(g_block, g_before, g_after)
        ge_sib = other_core(ge_own)
        gk, gv = attend_dkv(kv, qe_own, qe_sib, ge_own, ge_sib, where)
        g, ga_q, gb_q, gb_kv = qkv_back(
            gq, gk, gv, low_qkv, n1, a_first, b_q, b_kv, hidden_in, norm_gain[l, 0][None], gh2, wq, wkv
        )
        gb_q = [gb_q[:, :D], gb_kv[:, :D], gb_kv[:, WIDE : WIDE + D]]
        parts = eighths([ga_q, ga_o, ga_u, ga_d] + gb_q + [gb_o, gb_d], gb_u)
        if l > 0:
            parts, g = tie(parts, g)
            behind = sum_sequence(parts, core, y)

    got = lax.all_to_all(parts, BOTH, 0, 0, axis_index_groups=SAME_SEQUENCE)
    part = jnp.sum(got.astype(F32), axis=0).astype(BF)
    along_z = [lax.ppermute(part, BOTH, z_shift(by)) for by in (1, -1, 2)]
    behind, part = tie(behind, part)
    one = by_adapter([behind], picks_in_order)
    one, *along_z = tie(one, *along_z)
    one = lax.all_gather(one, BOTH, axis=0, axis_index_groups=SAME_SEQUENCE)
    along_z = jnp.stack([part] + along_z)
    before = lax.ppermute(along_z, "batch", x_shift(1))
    after = lax.ppermute(along_z, "batch", x_shift(-1))
    sent_home = theirs(g.reshape(2, HALF, D)), theirs(result.reshape(2, HALF, D))
    back_home = [lax.ppermute(a, "seq", SWAP) for a in sent_home]
    before, after, *back_home = tie(before, after, *back_home)
    far = [lax.ppermute(before[:2], "batch", x_shift(1)), lax.ppermute(after[2:], "batch", x_shift(-1))]
    whole = by_adapter([along_z, before, after] + far, picks_by_step)
    whole = whole.reshape(2, -1, 128)
    own = ring_far(whole, *ring_start(whole))
    one = unfold(unfold_late_kernel, 1, one)
    grad_tokens = halves(mine(g.reshape(2, HALF, D)), back_home[0])
    result = halves(mine(result.reshape(2, HALF, D)), back_home[1])
    own, grad_tokens, result, *one = tie(own, grad_tokens, result, *one)
    sib = other_core(own).reshape(4, PART, 128)
    ga_q, ga_o, ga_u, ga_d, gb_q, gb_o, gb_d, gb_u = unfold(
        unfold_kernel, 0, place_by_step, own.reshape(4, PART, 128), sib, one
    )
    gb_q, gb_o, gb_d = (jnp.swapaxes(a, 1, 2) for a in (gb_q, gb_o, gb_d))

    return result, grad_tokens, ga_q, gb_q, ga_o, gb_o, ga_u, gb_u, ga_d, gb_d


def solution(mesh):
    rows, flat, whole = P("batch", "seq", None), P(None, ("seq", "batch")), P()
    in_specs = (rows, P("batch", "seq"), P("batch"), whole) + (flat,) * 4 + (whole,) * 8 + (rows,)
    out_specs = (rows, rows) + (whole,) * 8
    return jax.shard_map(shards, mesh=mesh, in_specs=in_specs, out_specs=out_specs, check_vma=False)
```

profile of v0, /device:TPU:1, one launch (start us, length us, event | category | flops | bytes accessed | tf_op | source)
XLA Modules:
  0.0 517.0 jit_solution(7279070423683429013)
XLA Ops:
  79.8 9.9 %collective-permute-start.18 = (bf16[4,4,4,152,128]{4,3,2,1,0:T(8,128)(2,1)S(1)}, bf16[4,4,4,152,128]{4,3,2,1,0:T(8,128)(2,1)}, u32[]{:S(2)}, u32[]{:S(2)}) collective-permute-start(bf16[4,4,4,152,128]{4,3,2,1,0:T(8,128)(2,1)S(1)} %pad_maximum_fusion.1.own_2), channel_id=1, source_target_pairs={{0,8},{8,0},{16,24},{24,16},{32,40},{40,32},{48,56},{56,48},{64,72... | collective-permute-start | bytes 7471112 | tf_op jit(solution)/shard_map/ppermute | solution.py:496
  93.4 10.3 %collective-permute-start.13 = (bf16[4,4,4,152,128]{4,3,2,1,0:T(8,128)(2,1)}, bf16[4,4,4,152,128]{4,3,2,1,0:T(8,128)(2,1)}, u32[]{:S(2)}, u32[]{:S(2)}) collective-permute-start(bf16[4,4,4,152,128]{4,3,2,1,0:T(8,128)(2,1)} %pad_maximum_fusion.own_1), channel_id=1, source_target_pairs={{0,8},{8,0},{16,24},{24,16},{32,40},{40,32},{48,56},{56,48},{64,72... | collective-permute-start | bytes 7471112 | tf_op jit(solution)/shard_map/ppermute | solution.py:496
  112.3 12.8 %shard_map.276 = (bf16[1088,1152]{1,0:T(8,128)(2,1)S(1)}, bf16[1088,2304]{1,0:T(8,128)(2,1)S(1)}, bf16[1088,1088]{1,0:T(8,128)(2,1)S(1)}) custom-call(s32[13]{0:T(128)S(1)} %copy-done.59, bf16[4,4,4,152,128]{4,3,2,1,0:T(8,128)(2,1)} %pad_maximum_fusion.own_1, bf16[4,4,4,152,128]{4,3,2,1,0:T(8,128)(2,1)} %collective-permute-done.13.sib_1, ...), custom_call_target="tpu_custom_call" | custom-call | bytes 31457280 | tf_op jit(solution)/shard_map/pallas_call | solution.py:770
  132.9 13.1 %shard_map.277 = (bf16[1088,4352]{1,0:T(8,128)(2,1)S(1)}, bf16[4352,1088]{1,0:T(8,128)(2,1)S(1)}) custom-call(bf16[2,2,4,4,2,912,128]{6,5,4,3,2,1,0:T(8,128)(2,1)} %bitcast.313, bf16[2,2,4,4,2,912,128]{6,5,4,3,2,1,0:T(8,128)(2,1)} %bitcast.314), custom_call_target="tpu_custom_call" | custom-call | bytes 41943040 | tf_op jit(solution)/shard_map/pallas_call | solution.py:722
  153.7 9.7 %shard_map.278 = (bf16[1088,1152]{1,0:T(8,128)(2,1)S(1)}, bf16[1088,2304]{1,0:T(8,128)(2,1)S(1)}, bf16[1088,1088]{1,0:T(8,128)(2,1)S(1)}) custom-call(bf16[2,2,4,4,2,912,128]{6,5,4,3,2,1,0:T(8,128)(2,1)} %bitcast.315), custom_call_target="tpu_custom_call" | custom-call | bytes 20971520 | tf_op jit(solution)/shard_map/pallas_call | solution.py:722
  170.8 4.2 collective-permute-done.24.kv_sib
  175.0 8.2 %shard_map.279 = (bf16[128,1152]{1,0:T(8,128)(2,1)S(1)}, bf16[128,1152]{1,0:T(8,128)(2,1)S(1)}) custom-call(bf16[128,1152]{1,0:T(8,128)(2,1)S(1)} %fusion.5.q_ref, bf16[4,2,64,2304]{3,2,1,0:T(8,128)(2,1)} %pad_maximum_fusion.2.kv_own, bf16[4,2,64,2304]{3,2,1,0:T(8,128)(2,1)} %collective-permute-done.24.kv_sib, s32[128,1]{1,0:T(8,128)S(1)} %copy.151.lpos, ...), custom_call_target="tpu_custom_call" | custom-call | flops 8000000000 | bytes 6291456 | tf_op jit(solution)/shard_map/pallas_call | solution.py:231
  186.8 10.0 %shard_map.280 = (f32[128,1088]{1,0:T(8,128)S(1)}, bf16[128,1088]{1,0:T(8,128)(2,1)S(1)}, bf16[128,16]{1,0:T(8,128)(2,1)S(1)}, bf16[128,16]{1,0:T(8,128)(2,1)S(1...) custom-call(bf16[128,1152]{1,0:T(8,128)(2,1)S(1)} %get-tuple-element.209.ctx, ...), custom_call_target="tpu_custom_call" | custom-call | flops 10000000000 | bytes 25165824 | tf_op jit(solution)/shard_map/pallas_call | solution.py:435
  208.9 25.6 %collective-permute-done.30 = bf16[64,1152]{1,0:T(8,128)(2,1)S(1)} collective-permute-done((bf16[64,1152]{1,0:T(8,128)(2,1)S(1)}, bf16[64,1152]{1,0:T(8,128)(2,1)S(1)}, u32[]{:S(2)}, u32[]{:S(2)}) %collective-permute-start.30) | collective-permute-done | bytes 147488 | tf_op jit(solution)/shard_map/ppermute | solution.py:491
  240.7 6.0 %collective-permute-done.32 = bf16[64,2304]{1,0:T(8,128)(2,1)S(1)} collective-permute-done((bf16[64,2304]{1,0:T(8,128)(2,1)S(1)}, bf16[64,2304]{1,0:T(8,128)(2,1)S(1)}, u32[]{:S(2)}, u32[]{:S(2)}) %collective-permute-start.32) | collective-permute-done | bytes 294944 | tf_op jit(solution)/shard_map/ppermute | solution.py:491
  252.0 13.2 %shard_map.282 = (bf16[1088,4352]{1,0:T(8,128)(2,1)S(1)}, bf16[4352,1088]{1,0:T(8,128)(2,1)S(1)}) custom-call(bf16[2,2,4,4,2,608,128]{6,5,4,3,2,1,0:T(8,128)(2,1)} %bitcast.317, bf16[2,2,4,4,2,608,128]{6,5,4,3,2,1,0:T(8,128)(2,1)} %bitcast.318), custom_call_target="tpu_custom_call" | custom-call | bytes 41943040 | tf_op jit(solution)/shard_map/pallas_call | solution.py:722
  272.8 5.8 %shard_map.281 = (bf16[128,1152]{1,0:T(8,128)(2,1)S(1)}, bf16[128,1152]{1,0:T(8,128)(2,1)S(1)}) custom-call(bf16[128,1152]{1,0:T(8,128)(2,1)S(1)} %copy-done.20, bf16[4,2,64,2304]{3,2,1,0:T(8,128)(2,1)S(1)} %copy-done.9, bf16[4,2,64,2304]{3,2,1,0:T(8,128)(2,1)S(1)} %collective-permute-done.33.kv_sib, s32[128,1]{1,0:T(8,128)S(1)} %copy-done.36, ...), custom_call_target="tpu_custom_call" | custom-call | flops 8000000000 | bytes 6291456 | tf_op jit(solution)/shard_map/pallas_call | solution.py:231
  280.2 18.7 %shard_map.283 = (bf16[128,1088]{1,0:T(8,128)(2,1)S(1)}, f32[128,1088]{1,0:T(8,128)S(1)}, bf16[128,1152]{1,0:T(8,128)(2,1)S(1)}, bf16[16,1088]{1,0:T(8,128)(2,1)...) custom-call(bf16[128,1152]{1,0:T(8,128)(2,1)S(1)} %get-tuple-element, ...), custom_call_target="tpu_custom_call" | custom-call | flops 17999998976 | bytes 25165824 | tf_op jit(solution)/shard_map/pallas_call | solution.py:435
  309.3 7.1 %shard_map.284.gq = bf16[128,1152]{1,0:T(8,128)(2,1)S(1)} custom-call(bf16[128,1152]{1,0:T(8,128)(2,1)S(1)} %get-tuple-element.233.qe_ref, bf16[128,1152]{1,0:T(8,128)(2,1)S(1)} %get-tuple-element.259.ge_ref, bf16[4,2,64,2304]{3,2,1,0:T(8,128)(2,1)S(1)} %copy-done.9, bf16[4,2,64,2304]{3,2,1,0:T(8,128)(2,1)S(1)} %collective-permute-done.33.kv_sib, ...), custom_call_target="tpu_custom_call" | custom-call | flops 8000000000 | bytes 6291456 | tf_op jit(solution)/shard_map/pallas_call | solution.py:231
  331.0 10.5 %shard_map.285 = (bf16[2,64,1152]{2,1,0:T(8,128)(2,1)S(1)}, bf16[2,64,1152]{2,1,0:T(8,128)(2,1)S(1)}) custom-call(bf16[2,64,2304]{2,1,0:T(8,128)(2,1)S(1)} %bitcast.284, bf16[4,2,64,1152]{3,2,1,0:T(8,128)(2,1)} %pad_maximum_fusion.6.q_own, bf16[4,2,64,1152]{3,2,1,0:T(8,128)(2,1)} %collective-permute-done.40.q_sib, ...), custom_call_target="tpu_custom_call" | custom-call | flops 8000000000 | bytes 6291456 | tf_op jit(solution)/shard_map/pallas_call | solution.py:231
  341.5 4.6 shard_map.286
  352.9 17.3 %shard_map.287 = (f32[128,1088]{1,0:T(8,128)}, bf16[128,1152]{1,0:T(8,128)(2,1)}, bf16[16,1088]{1,0:T(8,128)(2,1)}, bf16[16,1088]{1,0:T(8,128)(2,1)}, bf16[16,10...) custom-call(f32[128,1088]{1,0:T(8,128)} %copy-done.71, ...), custom_call_target="tpu_custom_call" | custom-call | flops 16000000000 | bytes 25165824 | tf_op jit(solution)/shard_map/pallas_call | solution.py:435
  373.5 9.6 %shard_map.288.gq = bf16[128,1152]{1,0:T(8,128)(2,1)S(1)} custom-call(bf16[128,1152]{1,0:T(8,128)(2,1)S(1)} %copy-done.18, bf16[128,1152]{1,0:T(8,128)(2,1)S(1)} %copy-done.19, bf16[4,2,64,2304]{3,2,1,0:T(8,128)(2,1)} %pad_maximum_fusion.2.kv_own, bf16[4,2,64,2304]{3,2,1,0:T(8,128)(2,1)} %collective-permute-done.24.kv_sib, s32[128,1]{1,0:T(8,128)S(1)} %copy-done.37, ...), custom_call_target="tpu_custom_call" | custom-call | flops 8000000000 | bytes 6291456 | tf_op jit(solution)/shard_map/pallas_call | solution.py:231
  401.5 10.9 %shard_map.289 = (bf16[2,64,1152]{2,1,0:T(8,128)(2,1)S(1)}, bf16[2,64,1152]{2,1,0:T(8,128)(2,1)S(1)}) custom-call(bf16[2,64,2304]{2,1,0:T(8,128)(2,1)S(1)} %bitcast.280, bf16[4,2,64,1152]{3,2,1,0:T(8,128)(2,1)S(1)} %copy-done.10, bf16[4,2,64,1152]{3,2,1,0:T(8,128)(2,1)} %collective-permute-done.50.q_sib, bf16[4,2,64,1152]{3,2,1,0:T(8,128)(2,1)} %pad_maximum_fusion.8.g_own, ...), custom_call_target="tpu_custom_call" | custom-call | flops 8000000000 | bytes 6291456 | tf_op jit(solution)/shard_map/pallas_call | solution.py:231
  412.5 4.6 shard_map.290
  424.2 8.7 %all-to-all-done = bf16[8,16,2304]{2,1,0:T(8,128)(2,1)S(1)} async-done(((bf16[8,16,2304]{2,1,0:T(8,128)(2,1)}), bf16[8,16,2304]{2,1,0:T(8,128)(2,1)S(1)}, u32[]{:S(2)}, u32[]{:S(2)}) %all-to-all-start) | async-done | bytes 589856 | tf_op jit(solution)/shard_map/all_to_all | solution.py:953
  444.9 6.0 %collective-permute-done.60 = bf16[64,1088]{1,0:T(8,128)(2,1)S(1)} collective-permute-done((bf16[64,1088]{1,0:T(8,128)(2,1)S(1)}, bf16[64,1088]{1,0:T(8,128)(2,1)S(1)}, u32[]{:S(2)}, u32[]{:S(2)}) %collective-permute-start.60) | collective-permute-done | bytes 139296 | tf_op jit(solution)/shard_map/ppermute | solution.py:964
  461.0 20.3 %collective-permute-done.64 = bf16[2,1152,128]{2,1,0:T(8,128)(2,1)S(1)} collective-permute-done((bf16[2,1152,128]{2,1,0:T(8,128)(2,1)S(1)}, bf16[2,1152,128]{2,1,0:T(8,128)(2,1)S(1)}, u32[]{:S(2)}, u32[]{:S(2)}) %collective-permute-start.64) | collective-permute-done | bytes 589856 | tf_op jit(solution)/shard_map/ppermute | solution.py:486
  504.3 5.9 %shard_map.294 = (f32[2,1088,128]{2,1,0:T(8,128)}, f32[2,1088,128]{2,1,0:T(8,128)}, f32[2,1088,128]{2,1,0:T(8,128)}, f32[2,4352,128]{2,1,0:T(8,128)}, f32[2,3264...) custom-call(s32[8]{0:T(128)S(1)} %fusion.44.place, ...), custom_call_target="tpu_custom_call", output_to_operand_aliasing={{0}: (3, {}), {1}: (4, {}), {2}: (5, {}), {3}: (6, {}), {4}... | custom-call | bytes 14680064 | tf_op jit(solution)/shard_map/pallas_call | solution.py:596
  (609 shorter events, 246.9 us)
Async XLA Ops:
  7.2 125.7 %all-gather.8.cloned.1.call-start = ((), (), s32[]{:S(2)}) async-start(), calls=%async_computation.1 | async-start | bytes 30117888 | tf_op jit(solution)/shard_map/all_gather | solution.py:814
  15.1 234.5 %all-gather.10.cloned.1.call-start = ((), (), s32[]{:S(2)}) async-start(), calls=%async_computation.2 | async-start | bytes 20078592 | tf_op jit(solution)/shard_map/all_gather | solution.py:814
  15.9 418.8 %all-gather.12.cloned.1.call-start = ((), (), s32[]{:S(2)}) async-start(), calls=%async_computation.3 | async-start | bytes 2506752 | tf_op jit(solution)/shard_map/all_gather | solution.py:938
  39.3 31.1 %collective-permute-start.19 = (bf16[2,64,1088]{2,1,0:T(8,128)(2,1)}, bf16[2,64,1088]{2,1,0:T(8,128)(2,1)}, u32[]{:S(2)}, u32[]{:S(2)}) collective-permute-start(bf16[2,64,1088]{2,1,0:T(8,128)(2,1)} %pad_maximum_fusion.12), channel_id=1, source_target_pairs={{0,64},{8,72},{16,80},{24,88},{32,96},{40,104},{48,112},{56,120},{... | collective-permute-start | bytes 835592 | tf_op jit(solution)/shard_map/ppermute | solution.py:822
  43.9 27.7 %collective-permute-start.10 = (bf16[4,4,152,128]{3,2,1,0:T(8,128)(2,1)S(1)}, bf16[4,4,152,128]{3,2,1,0:T(8,128)(2,1)}, u32[]{:S(2)}, u32[]{:S(2)}) collective-permute-start(bf16[4,4,152,128]{3,2,1,0:T(8,128)(2,1)S(1)} %pad_maximum_fusion.9), channel_id=1, source_target_pairs={{0,65},{8,73},{2,67},{10,75},{4,69},{12,77},{6,71},{14,79},{16,81}... | collective-permute-start | bytes 1867784 | tf_op jit(solution)/shard_map/ppermute | solution.py:747
  46.6 28.8 %collective-permute-start.9 = (bf16[4,4,152,128]{3,2,1,0:T(8,128)(2,1)S(1)}, bf16[4,4,152,128]{3,2,1,0:T(8,128)(2,1)}, u32[]{:S(2)}, u32[]{:S(2)}) collective-permute-start(bf16[4,4,152,128]{3,2,1,0:T(8,128)(2,1)S(1)} %pad_maximum_fusion.9), channel_id=1, source_target_pairs={{0,1},{8,9},{2,3},{10,11},{4,5},{12,13},{6,7},{14,15},{16,17},{24,... | collective-permute-start | bytes 1867784 | tf_op jit(solution)/shard_map/ppermute | solution.py:746
  46.6 19.5 %collective-permute-start.15 = (bf16[4,4,152,128]{3,2,1,0:T(8,128)(2,1)S(1)}, bf16[4,4,152,128]{3,2,1,0:T(8,128)(2,1)}, u32[]{:S(2)}, u32[]{:S(2)}) collective-permute-start(bf16[4,4,152,128]{3,2,1,0:T(8,128)(2,1)S(1)} %pad_maximum_fusion.10), channel_id=1, source_target_pairs={{0,48},{8,56},{16,0},{24,8},{32,16},{40,24},{48,32},{56,40},{64,11... | collective-permute-start | bytes 1867784 | tf_op jit(solution)/shard_map/ppermute | solution.py:747
  47.7 21.7 %collective-permute-start.14 = (bf16[4,4,152,128]{3,2,1,0:T(8,128)(2,1)S(1)}, bf16[4,4,152,128]{3,2,1,0:T(8,128)(2,1)}, u32[]{:S(2)}, u32[]{:S(2)}) collective-permute-start(bf16[4,4,152,128]{3,2,1,0:T(8,128)(2,1)S(1)} %pad_maximum_fusion.10), channel_id=1, source_target_pairs={{0,16},{8,24},{16,32},{24,40},{32,48},{40,56},{48,0},{56,8},{64,80... | collective-permute-start | bytes 1867784 | tf_op jit(solution)/shard_map/ppermute | solution.py:746
  79.8 27.1 %collective-permute-start.18 = (bf16[4,4,4,152,128]{4,3,2,1,0:T(8,128)(2,1)S(1)}, bf16[4,4,4,152,128]{4,3,2,1,0:T(8,128)(2,1)}, u32[]{:S(2)}, u32[]{:S(2)}) collective-permute-start(bf16[4,4,4,152,128]{4,3,2,1,0:T(8,128)(2,1)S(1)} %pad_maximum_fusion.1.own_2), channel_id=1, source_target_pairs={{0,8},{8,0},{16,24},{24,16},{32,40},{40,32},{48,56},{56,48},{64,72... | collective-permute-start | bytes 7471112 | tf_op jit(solution)/shard_map/ppermute | solution.py:496
  93.4 18.3 %collective-permute-start.13 = (bf16[4,4,4,152,128]{4,3,2,1,0:T(8,128)(2,1)}, bf16[4,4,4,152,128]{4,3,2,1,0:T(8,128)(2,1)}, u32[]{:S(2)}, u32[]{:S(2)}) collective-permute-start(bf16[4,4,4,152,128]{4,3,2,1,0:T(8,128)(2,1)} %pad_maximum_fusion.own_1), channel_id=1, source_target_pairs={{0,8},{8,0},{16,24},{24,16},{32,40},{40,32},{48,56},{56,48},{64,72... | collective-permute-start | bytes 7471112 | tf_op jit(solution)/shard_map/ppermute | solution.py:496
  128.9 20.9 %collective-permute-start.21 = (bf16[2,64,2304]{2,1,0:T(8,128)(2,1)S(1)}, bf16[2,64,2304]{2,1,0:T(8,128)(2,1)S(1)}, u32[]{:S(2)}, u32[]{:S(2)}) collective-permute-start(bf16[2,64,2304]{2,1,0:T(8,128)(2,1)S(1)} %bitcast.277), channel_id=1, source_target_pairs={{0,48},{8,56},{16,0},{24,8},{32,16},{40,24},{48,32},{56,40},{64,11... | collective-permute-start | bytes 1769480 | tf_op jit(solution)/shard_map/ppermute | solution.py:486
  204.2 34.9 %collective-permute-start.28 = (bf16[2,64,2304]{2,1,0:T(8,128)(2,1)S(1)}, bf16[2,64,2304]{2,1,0:T(8,128)(2,1)S(1)}, u32[]{:S(2)}, u32[]{:S(2)}) collective-permute-start(bf16[2,64,2304]{2,1,0:T(8,128)(2,1)S(1)} %bitcast.281), channel_id=1, source_target_pairs={{0,48},{8,56},{16,0},{24,8},{32,16},{40,24},{48,32},{56,40},{64,11... | collective-permute-start | bytes 1769480 | tf_op jit(solution)/shard_map/ppermute | solution.py:486
  204.3 34.8 %collective-permute-start.27 = (bf16[2,64,2304]{2,1,0:T(8,128)(2,1)S(1)}, bf16[2,64,2304]{2,1,0:T(8,128)(2,1)S(1)}, u32[]{:S(2)}, u32[]{:S(2)}) collective-permute-start(bf16[2,64,2304]{2,1,0:T(8,128)(2,1)S(1)} %bitcast.282), channel_id=1, source_target_pairs={{0,16},{8,24},{16,32},{24,40},{32,48},{40,56},{48,0},{56,8},{64,80... | collective-permute-start | bytes 1769480 | tf_op jit(solution)/shard_map/ppermute | solution.py:486
  205.8 28.8 %collective-permute-start.30 = (bf16[64,1152]{1,0:T(8,128)(2,1)S(1)}, bf16[64,1152]{1,0:T(8,128)(2,1)S(1)}, u32[]{:S(2)}, u32[]{:S(2)}) collective-permute-start(bf16[64,1152]{1,0:T(8,128)(2,1)S(1)} %slice_bitcast_fusion.13), channel_id=1, source_target_pairs={{0,48},{8,56},{16,0},{24,8},{32,16},{40,24},{48,32},{56,40},{64,11... | collective-permute-start | bytes 442376 | tf_op jit(solution)/shard_map/ppermute | solution.py:491
  207.1 30.7 %collective-permute-start.29 = (bf16[64,1152]{1,0:T(8,128)(2,1)S(1)}, bf16[64,1152]{1,0:T(8,128)(2,1)S(1)}, u32[]{:S(2)}, u32[]{:S(2)}) collective-permute-start(bf16[64,1152]{1,0:T(8,128)(2,1)S(1)} %slice_bitcast_fusion.14), channel_id=1, source_target_pairs={{0,16},{8,24},{16,32},{24,40},{32,48},{40,56},{48,0},{56,8},{64,80... | collective-permute-start | bytes 442376 | tf_op jit(solution)/shard_map/ppermute | solution.py:490
  249.6 23.2 %collective-permute-start.33 = (bf16[4,2,64,2304]{3,2,1,0:T(8,128)(2,1)}, bf16[4,2,64,2304]{3,2,1,0:T(8,128)(2,1)S(1)}, u32[]{:S(2)}, u32[]{:S(2)}) collective-permute-start(bf16[4,2,64,2304]{3,2,1,0:T(8,128)(2,1)} %pad_maximum_fusion.3.kv_own), channel_id=1, source_target_pairs={{0,8},{8,0},{16,24},{24,16},{32,40},{40,32},{48,56},{56,48},{64,72... | collective-permute-start | bytes 7077896 | tf_op jit(solution)/shard_map/ppermute | solution.py:496
  278.6 20.4 %collective-permute-start.35 = (bf16[2,64,1152]{2,1,0:T(8,128)(2,1)S(1)}, bf16[2,64,1152]{2,1,0:T(8,128)(2,1)S(1)}, u32[]{:S(2)}, u32[]{:S(2)}) collective-permute-start(bf16[2,64,1152]{2,1,0:T(8,128)(2,1)S(1)} %bitcast.301), channel_id=1, source_target_pairs={{0,48},{8,56},{16,0},{24,8},{32,16},{40,24},{48,32},{56,40},{64,11... | collective-permute-start | bytes 884744 | tf_op jit(solution)/shard_map/ppermute | solution.py:486
  278.7 20.3 %collective-permute-start.34 = (bf16[2,64,1152]{2,1,0:T(8,128)(2,1)S(1)}, bf16[2,64,1152]{2,1,0:T(8,128)(2,1)S(1)}, u32[]{:S(2)}, u32[]{:S(2)}) collective-permute-start(bf16[2,64,1152]{2,1,0:T(8,128)(2,1)S(1)} %bitcast.302), channel_id=1, source_target_pairs={{0,16},{8,24},{16,32},{24,40},{32,48},{40,56},{48,0},{56,8},{64,80... | collective-permute-start | bytes 884744 | tf_op jit(solution)/shard_map/ppermute | solution.py:486
  349.7 22.0 %collective-permute-start.45 = (bf16[16,2304]{1,0:T(8,128)(2,1)S(1)}, bf16[16,2304]{1,0:T(8,128)(2,1)S(1)}, u32[]{:S(2)}, u32[]{:S(2)}) collective-permute-start(bf16[16,2304]{1,0:T(8,128)(2,1)S(1)} %get-tuple-element.354), channel_id=1, source_target_pairs={{0,16},{8,24},{16,32},{24,40},{32,48},{40,56},{48,0},{56,8},{64,80... | collective-permute-start | bytes 221192 | tf_op jit(solution)/shard_map/ppermute | solution.py:510
  349.8 22.0 %collective-permute-start.47 = (bf16[16,2304]{1,0:T(8,128)(2,1)S(1)}, bf16[16,2304]{1,0:T(8,128)(2,1)S(1)}, u32[]{:S(2)}, u32[]{:S(2)}) collective-permute-start(bf16[16,2304]{1,0:T(8,128)(2,1)S(1)} %get-tuple-element.355), channel_id=1, source_target_pairs={{0,32},{8,40},{16,48},{24,56},{32,0},{40,8},{48,16},{56,24},{64,96... | collective-permute-start | bytes 221192 | tf_op jit(solution)/shard_map/ppermute | solution.py:510
  350.7 21.1 %collective-permute-start.46 = (bf16[16,2304]{1,0:T(8,128)(2,1)S(1)}, bf16[16,2304]{1,0:T(8,128)(2,1)S(1)}, u32[]{:S(2)}, u32[]{:S(2)}) collective-permute-start(bf16[16,2304]{1,0:T(8,128)(2,1)S(1)} %get-tuple-element.356), channel_id=1, source_target_pairs={{0,48},{8,56},{16,0},{24,8},{32,16},{40,24},{48,32},{56,40},{64,11... | collective-permute-start | bytes 221192 | tf_op jit(solution)/shard_map/ppermute | solution.py:510
  422.7 68.2 %all-gather.14.cloned.1.call-start = ((), (), s32[]{:S(2)}) async-start(), calls=%async_computation.4 | async-start | bytes 5308416 | tf_op jit(solution)/shard_map/all_gather | solution.py:959
  459.4 21.9 %collective-permute-start.64 = (bf16[2,1152,128]{2,1,0:T(8,128)(2,1)S(1)}, bf16[2,1152,128]{2,1,0:T(8,128)(2,1)S(1)}, u32[]{:S(2)}, u32[]{:S(2)}) collective-permute-start(bf16[2,1152,128]{2,1,0:T(8,128)(2,1)S(1)} %bitcast.285), channel_id=1, source_target_pairs={{0,48},{8,56},{16,0},{24,8},{32,16},{40,24},{48,32},{56,40},{64,11... | collective-permute-start | bytes 1769480 | tf_op jit(solution)/shard_map/ppermute | solution.py:486
  460.4 22.3 %collective-permute-start.63 = (bf16[2,1152,128]{2,1,0:T(8,128)(2,1)S(1)}, bf16[2,1152,128]{2,1,0:T(8,128)(2,1)S(1)}, u32[]{:S(2)}, u32[]{:S(2)}) collective-permute-start(bf16[2,1152,128]{2,1,0:T(8,128)(2,1)S(1)} %bitcast.286), channel_id=1, source_target_pairs={{0,16},{8,24},{16,32},{24,40},{32,48},{40,56},{48,0},{56,8},{64,80... | collective-permute-start | bytes 1769480 | tf_op jit(solution)/shard_map/ppermute | solution.py:486
  (178 other events, 1880.1 us)
Sparse Core Ops, SparseCore 0:
  15.2 117.0 all-gather.7
  135.3 103.4 all-gather.9
  389.0 42.1 all-gather.11
  439.4 38.8 all-gather.13
where the time goes:
time: 525 us; the launch traced here: 517 us
  Pallas kernels  169 us (32%)
  waiting for transfers between devices  115 us (22%)
  starting transfers between devices  106 us (20%)
  local copies, waits for them, and re-layouts  69.4 us (13%)
  other arithmetic  35.5 us (7%)
  between operations  17 us (3%)
    pallas_call x6, Pallas kernels, attention_call(): pl.pallas_call(kernel, out_shape=outs, in_specs=[HERE] * len(args), out_s...  52 us
    pallas_call x3, Pallas kernels, mlp_call(): pl.pallas_call(kernel, out_shape=outs, in_specs=[HERE] * (len(args) - 3)...  46 us
    ppermute x7, waiting for transfers between devices, ring_far(): far_hi = lax.ppermute(after[1], 'seq', DOWN)  38.9 us
    ppermute x9, starting transfers between devices, other_core(): return lax.ppermute(own, 'seq', CORE)  37.4 us
    pallas_call x3, Pallas kernels, unpack(): pl.pallas_call(kernel, grid=(8,), out_shape=tuple((jax.ShapeDtypeStruct((...  36.1 us
    unnamed x264, local copies, waits for them, and re-layouts  26.4 us
    ppermute x14, waiting for transfers between devices, ring_start(): return (lax.ppermute(block, 'seq', UP), lax.ppermute(block, 'seq', DOWN))  25.6 us
    ppermute x7, waiting for transfers between devices, ring_far(): far_lo = lax.ppermute(before[0], 'seq', UP)  14.5 us
  transfers between devices with their start and end apart: 73, of which 25 were waited for; matrix products, arithmetic and copies ran while one was open for 14% of the time, Pallas kernels for 27%

commit v1 on v0

--- a/solution.py
+++ b/solution.py
@@ -221,7 +221,7 @@
 ATTENTION_COST = pl.CostEstimate(
     flops=8_000_000_000, bytes_accessed=6 << 20, transcendentals=PAIRS * 256 * KEYS
 )
-PARAMS = pltpu.CompilerParams(vmem_limit_bytes=24 * 1024 * 1024)
+PARAMS = pltpu.CompilerParams(vmem_limit_bytes=17 * 1024 * 1024)
 HERE = pl.BlockSpec(memory_space=pltpu.VMEM)
 ANYWHERE = pl.BlockSpec(memory_space=pl.ANY)
 FLAT = jax.ShapeDtypeStruct((2 * HALF, WIDE), BF)
@@ -274,30 +274,22 @@
 
 def mlp_fwd_kernel(
     ctx, hidden, gain, gain_next, a_o, b_o, a_u, b_d, b_u, a_d, wout, wup, wdown,
-    middle, n2, low_o, low_u, low_d, after, n1_next, wout_here, wup_here, wdown_here, sems
+    middle, n2, low_o, low_u, low_d, after, n1_next
 ):
-    out, ups, downs = weight_copies(FWD_PIECES, wout, wup, wdown, wout_here, wup_here, wdown_here, sems)
-    out.start()
-    for up, down in zip(ups, downs):
-        up.start()
-        down.start()
     x = ctx[:, :D]
     low = dot(x, a_o[...]).astype(BF)
     low_o[...] = low
-    out.wait()
-    mid = hidden[...] + dot(x, wout_here[...]) + dot(low, b_o[...])
+    mid = hidden[...] + dot(x, wout[...]) + dot(low, b_o[...])
     middle[...] = mid
     normed = (normalised(mid)[0] * gain[...]).astype(BF)
     n2[...] = normed
     low = dot(normed, a_u[...]).astype(BF)
     low_u[...] = low
     total, total_low = jnp.zeros((ROWS, D), F32), jnp.zeros((ROWS, RANK), F32)
-    for k, (a, b) in enumerate(FWD_PIECES):
-        ups[k].wait()
-        up = dot(normed, wup_here[:, a:b]) + dot(low, b_u[:, a:b])
+    for a, b in FWD_PIECES:
+        up = dot(normed, wup[:, a:b]) + dot(low, b_u[:, a:b])
         act = (up * (0.5 * (1.0 + lax.erf(up * 0.7071067811865476)))).astype(BF)
-        downs[k].wait()
-        total = total + dot(act, wdown_here[a:b, :])
+        total = total + dot(act, wdown[a:b, :])
         total_low = total_low + dot(act, a_d[a:b, :])
     low = total_low.astype(BF)
     low_d[...] = low
@@ -386,37 +378,29 @@
 
 def mlp_both_kernel(
     ctx, hidden, gain, g, a_o, b_o, a_u, b_d, spread, b_u, a_d, wout, wup, wdown,
-    after, gh2, ge, ga_o, gb_o, ga_u, gb_d, ga_d, gb_u, wout_here, wup_here, wdown_here, sems
+    after, gh2, ge, ga_o, gb_o, ga_u, gb_d, ga_d, gb_u
 ):
-    out, ups, downs = weight_copies(BACK_PIECES, wout, wup, wdown, wout_here, wup_here, wdown_here, sems)
-    out.start()
-    for up, down in zip(ups, downs):
-        up.start()
-        down.start()
     x = ctx[:, :D]
     low_o = dot(x, a_o[...]).astype(BF)
-    out.wait()
-    gh2[...] = hidden[...] + dot(x, wout_here[...]) + dot(low_o, b_o[...])
+    gh2[...] = hidden[...] + dot(x, wout[...]) + dot(low_o, b_o[...])
     normed = (normalised(gh2[...])[0] * gain[...]).astype(BF)
     low = dot(normed, a_u[...]).astype(BF)
     gy = g[...].astype(BF)
     glow_d = dot_t(gy, b_d[...]).astype(BF)
     total, total_low = jnp.zeros((ROWS, D), F32), jnp.zeros((ROWS, RANK), F32)
     gn2, glow_u = jnp.zeros((ROWS, D), F32), jnp.zeros((ROWS, RANK), F32)
-    for k, (a, b) in enumerate(BACK_PIECES):
-        ups[k].wait()
-        up = dot(normed, wup_here[:, a:b]) + dot(low, b_u[:, a:b])
+    for a, b in BACK_PIECES:
+        up = dot(normed, wup[:, a:b]) + dot(low, b_u[:, a:b])
         phi = 0.5 * (1.0 + lax.erf(up * 0.7071067811865476))
         act = (up * phi).astype(BF)
         ga_d[:, a:b] = t_dot(glow_d, act).astype(BF)
-        downs[k].wait()
-        total = total + dot(act, wdown_here[a:b, :])
+        total = total + dot(act, wdown[a:b, :])
         total_low = total_low + dot(act, a_d[a:b, :])
-        gact = dot_t(gy, wdown_here[a:b, :]) + dot_t(glow_d, a_d[a:b, :])
+        gact = dot_t(gy, wdown[a:b, :]) + dot_t(glow_d, a_d[a:b, :])
         density = jnp.exp(-0.5 * up * up) * 0.3989422804014327
         gup = (gact * (phi + up * density)).astype(BF)
         gb_u[:, a:b] = t_dot(low, gup).astype(BF)
-        gn2 = gn2 + dot_t(gup, wup_here[:, a:b])
+        gn2 = gn2 + dot_t(gup, wup[:, a:b])
         glow_u = glow_u + dot_t(gup, b_u[:, a:b])
     low_d = total_low.astype(BF)
     gb_d[...] = t_dot(low_d, gy).astype(BF)
@@ -424,25 +408,26 @@
     glow_u = glow_u.astype(BF)
     gn2 = gn2 + dot_t(glow_u, a_u[...])
     ga_u[...] = t_dot(glow_u, normed).astype(BF)
-    through_norm(g, gh2[...], gain, gn2, x, low_o, a_o, b_o, wout_here, spread, gh2, ge, ga_o, gb_o)
+    through_norm(g, gh2[...], gain, gn2, x, low_o, a_o, b_o, wout, spread, gh2, ge, ga_o, gb_o)
 
 
 def shape_of(rows, width, kind=BF):
     return jax.ShapeDtypeStruct((rows, width), kind)
 
 
-def mlp_call(kernel, pieces, args, outs, flops, limit=40):
+def mlp_call(kernel, args, outs, flops, weights=0, limit=24):
+    scratch = [
+        pltpu.VMEM((D, D), BF),
+        pltpu.VMEM((D, FF), BF),
+        pltpu.VMEM((FF, D), BF),
+        pltpu.SemaphoreType.DMA((1 + 2 * len(BACK_PIECES),)),
+    ]
     return pl.pallas_call(
         kernel,
         out_shape=outs,
-        in_specs=[HERE] * (len(args) - 3) + [ANYWHERE] * 3,
+        in_specs=[HERE] * (len(args) - weights) + [ANYWHERE] * weights,
         out_specs=(HERE,) * len(outs),
-        scratch_shapes=[
-            pltpu.VMEM((D, D), BF),
-            pltpu.VMEM((D, FF), BF),
-            pltpu.VMEM((FF, D), BF),
-            pltpu.SemaphoreType.DMA((1 + 2 * len(pieces),)),
-        ],
+        scratch_shapes=scratch if weights else (),
         compiler_params=pltpu.CompilerParams(vmem_limit_bytes=limit * 1024 * 1024),
         cost_estimate=pl.CostEstimate(flops=flops, bytes_accessed=24 << 20, transcendentals=ROWS * FF),
     )(*args)
@@ -451,13 +436,19 @@
 def mlp_fwd(*args):
     outs = (shape_of(ROWS, D, F32), shape_of(ROWS, D)) + (shape_of(ROWS, RANK),) * 3
     outs += (shape_of(ROWS, D, F32), shape_of(ROWS, D))
-    return mlp_call(mlp_fwd_kernel, FWD_PIECES, args, outs, 10_000_000_000)
+    return mlp_call(mlp_fwd_kernel, args, outs, 10_000_000_000, limit=12)
 
 
 def mlp_both(*args):
     outs = (shape_of(ROWS, D), shape_of(ROWS, D, F32), shape_of(ROWS, WIDE)) + (shape_of(RANK, D),) * 4
     outs += (shape_of(RANK, FF),) * 2
-    return mlp_call(mlp_both_kernel, BACK_PIECES, args, outs, 18_000_000_000)
+    return mlp_call(mlp_both_kernel, args, outs, 18_000_000_000, limit=20)
+
+
+def mlp_back(*args):
+    outs = (shape_of(ROWS, D, F32), shape_of(ROWS, WIDE)) + (shape_of(RANK, D),) * 4
+    outs += (shape_of(RANK, FF),) * 2
+    return mlp_call(mlp_back_kernel, args, outs, 16_000_000_000, 3, 56)
 
 
 def qkv_back(*args):
@@ -476,20 +467,16 @@
     )(*args)
 
 
-def mlp_back(*args):
-    outs = (shape_of(ROWS, D, F32), shape_of(ROWS, WIDE)) + (shape_of(RANK, D),) * 4
-    outs += (shape_of(RANK, FF),) * 2
-    return mlp_call(mlp_back_kernel, BACK_PIECES, args, outs, 16_000_000_000, 56)
-
-
 def ring_start(block):
     return lax.ppermute(block, "seq", UP), lax.ppermute(block, "seq", DOWN)
 
 
-def ring_far(block, before, after):
+def ring_far(block, before, after, beside=()):
     far_lo = lax.ppermute(before[0], "seq", UP)
     far_hi = lax.ppermute(after[1], "seq", DOWN)
-    return jnp.stack([block, before, after, jnp.stack([far_lo, far_hi])])
+    far_lo, far_hi, *beside = tie(far_lo, far_hi, *beside)
+    own = jnp.stack([block, before, after, jnp.stack([far_lo, far_hi])])
+    return (own, *beside) if beside else own
 
 
 def other_core(own):
@@ -713,7 +700,7 @@
         columns(s_down, down_ref, 128 * j, 2 * j, 17)
 
 
-def unpack(kernel, got, at, outs, scratch_lines):
+def unpack(kernel, got, at, outs, scratch_lines, limit):
     g = got.reshape(2, 2, 4, 4, 2, -1, 128)
 
     def spec(k):
@@ -726,7 +713,7 @@
         in_specs=[spec(k) for k in at],
         out_specs=tuple(pl.BlockSpec((r, w), lambda i: (i, 0)) for r, w in outs),
         scratch_shapes=[pltpu.VMEM((n, 128), F32) for n in scratch_lines],
-        compiler_params=pltpu.CompilerParams(vmem_limit_bytes=26 * 1024 * 1024),
+        compiler_params=pltpu.CompilerParams(vmem_limit_bytes=limit * 1024 * 1024),
         cost_estimate=pl.CostEstimate(
             flops=0, bytes_accessed=len(at) * (20 << 20), transcendentals=0
         ),
@@ -738,7 +725,7 @@
 
 
 def unpack_attention(got, at):
-    return unpack(unpack_attention_kernel, got, [at], ATTENTION_OUTS, ATTENTION_LINES)
+    return unpack(unpack_attention_kernel, got, [at], ATTENTION_OUTS, ATTENTION_LINES, 36)
 
 
 def along(axis, block, near):
@@ -784,7 +771,7 @@
 
 def unpack_mlp(got, at):
     outs = [(BLOCK, FF), (4 * BLOCK, D)]
-    return unpack(unpack_mlp_kernel, got, [at, at + 1], outs, [16 * N_UP, 32 * N_DOWN + 8])
+    return unpack(unpack_mlp_kernel, got, [at, at + 1], outs, [16 * N_UP, 32 * N_DOWN + 8], 20)
 
 
 def shards(
@@ -887,35 +874,29 @@
         q = (dot(n1, wq) + dot(low_qkv, b_q)).astype(BF) * jnp.asarray(0.125, BF)
         before, after = ring_start(kv)
         if l == 0:
-            wup, wdown = unpack_mlp(early, 0)
-            before, after, q, wup, wdown = tie(before, after, q, wup, wdown)
+            before, after, q, wup, wdown = tie(before, after, q, *unpack_mlp(early, 0))
         else:
-            before, after, q, qe_own = tie(before, after, q, qe_own)
-            queries.append((qe_own, other_core(qe_own)))
-        kv_own = ring_far(kv, before, after)
-        if l > 0:
-            late, kv_own = tie(late, kv_own)
-            wup, wdown = unpack_mlp(late, 0)
+            before, after, q, late = tie(before, after, q, late)
         if l == 0:
-            first = unpack_attention(early, 2)
-            kv_own, *first = tie(kv_own, *first)
+            kv_own, *first = ring_far(kv, before, after, unpack_attention(early, 2))
+        else:
+            kv_own, wup, wdown = ring_far(kv, before, after, unpack_mlp(late, 0))
         kv_sib = other_core(kv_own)
         ctx, qe = attend_fwd(q, kv_own, kv_sib, where)
-        qe = qe.reshape(2, HALF, WIDE)
-        q_before, q_after = ring_start(qe)
+        queries.append(qe.reshape(2, HALF, WIDE))
         gains = norm_gain[l, 1][None], norm_gain[(l + 1) % layers, 0][None]
         small, large = (a_o, b_o, a_u, b_d), (b_u, a_d, wout, wup, wdown)
         rows, hidden_next, n1_next = None, None, None
         if l < layers - 1:
             middle, n2, low_o, low_u, low_d, hidden_next, n1_next = mlp_fwd(ctx, hidden, *gains, *small, *large)
-            q_before, q_after, hidden_next, n1_next = tie(q_before, q_after, hidden_next, n1_next)
             rows = (ctx, middle, gains[0], n2, low_o, low_u, low_d)
         else:
+            starts = [ring_start(a) for a in queries]
             result, *back = mlp_both(ctx, hidden, gains[0], grad_hidden, *small, spread, *large)
-            q_before, q_after, *back = tie(q_before, q_after, *back)
-        qe_own = ring_far(qe, q_before, q_after)
+            starts, back = tie(starts, back)
+            queries = [ring_far(a, *start) for a, start in zip(queries, starts)]
         saved.append(
-            (hidden, n1, low_qkv, kv, kv_own, kv_sib, qe.reshape(2 * HALF, WIDE))
+            (hidden, n1, low_qkv, kv, kv_own, kv_sib, qe)
             + (rows, small, large, a_first, b_q, b_kv, wq, wkv)
         )
         hidden, n1 = hidden_next, n1_next
@@ -927,10 +908,8 @@
             back = mlp_back(g, *rows, *small, spread, *large)
         gh2, ge, ga_o, gb_o, ga_u, gb_d, ga_d, gb_u = back
         if l == layers - 1:
-            qe_own, ge = tie(qe_own, ge)
-            qe_sib = other_core(qe_own)
-        else:
-            qe_own, qe_sib = queries[l]
+            queries, ge = tie(queries, ge)
+        qe_own, qe_sib = queries[l], other_core(queries[l])
         g_block = ge.reshape(2, HALF, WIDE)
         g_before, g_after = ring_start(g_block)
         if behind is not None:
@@ -962,7 +941,6 @@
     after = lax.ppermute(along_z, "batch", x_shift(-1))
     sent_home = theirs(g.reshape(2, HALF, D)), theirs(result.reshape(2, HALF, D))
     back_home = [lax.ppermute(a, "seq", SWAP) for a in sent_home]
-    before, after, *back_home = tie(before, after, *back_home)
     far = [lax.ppermute(before[:2], "batch", x_shift(1)), lax.ppermute(after[2:], "batch", x_shift(-1))]
     whole = by_adapter([along_z, before, after] + far, picks_by_step)
     whole = whole.reshape(2, -1, 128)

time: 525 us -> 514 us (0.979)
  waiting for transfers between devices: 115 us -> 83.9 us
  starting transfers between devices: 106 us -> 123 us
  local copies, waits for them, and re-layouts: 69.4 us -> 76.7 us
  Pallas kernels: 169 us -> 162 us
    ppermute x7, waiting for transfers between devices: 38.9 us -> 0.02 us  [ring_far(): far_hi = lax.ppermute(after[1], 'seq', DOWN)]
    all_gather x2, waiting for transfers between devices: 0.02 us -> 11.7 us  [gather(): return lax.all_gather(a, BOTH, axis=0, tiled=True, axis_index_groups=ALL)]
    ppermute x7, waiting for transfers between devices: 14.5 us -> 5.14 us  [ring_far(): far_lo = lax.ppermute(before[0], 'seq', UP)]
    ppermute x7, starting transfers between devices: 10.9 us -> 18.8 us  [ring_far(): far_hi = lax.ppermute(after[1], 'seq', DOWN)]
    pallas_call x3, Pallas kernels: 46 us -> 39.4 us  [mlp_call(): pl.pallas_call(kernel, out_shape=outs, in_specs=[HERE] * (len(args) - wei...]
    ppermute x2, waiting for transfers between devices: 6.04 us -> 0.01 us  [shards(): back_home = [lax.ppermute(a, 'seq', SWAP) for a in sent_home]]
    unnamed x264 -> x266, local copies, waits for them, and re-layouts: 26.4 us -> 32.1 us
    ppermute x9, starting transfers between devices: 37.4 us -> 31.9 us  [other_core(): return lax.ppermute(own, 'seq', CORE)]
  transfers between devices with their start and end apart: 73 -> 73, of which waited for: 25 -> 17; matrix products, arithmetic and copies ran while one was open for 14% -> 14% of each run, Pallas kernels for 27% -> 27%
where the time goes in v1:
time: 514 us; the launch traced here: 506 us
  Pallas kernels  162 us (32%)
  starting transfers between devices  123 us (24%)
  waiting for transfers between devices  83.9 us (16%)
  local copies, waits for them, and re-layouts  76.7 us (15%)
  other arithmetic  38.1 us (7%)
  between operations  17 us (3%)
  matrix products  5.27 us (1%)
    pallas_call x6, Pallas kernels, attention_call(): pl.pallas_call(kernel, out_shape=outs, in_specs=[HERE] * len(args), out_s...  52 us
    pallas_call x3, Pallas kernels, mlp_call(): pl.pallas_call(kernel, out_shape=outs, in_specs=[HERE] * (len(args) - wei...  39.4 us
    pallas_call x3, Pallas kernels, unpack(): pl.pallas_call(kernel, grid=(8,), out_shape=tuple((jax.ShapeDtypeStruct((...  35.9 us
    unnamed x266, local copies, waits for them, and re-layouts  32.1 us
    ppermute x9, starting transfers between devices, other_core(): return lax.ppermute(own, 'seq', CORE)  31.9 us
    ppermute x14, waiting for transfers between devices, ring_start(): return (lax.ppermute(block, 'seq', UP), lax.ppermute(block, 'seq', DOWN))  27.5 us
    ppermute x14, starting transfers between devices, ring_start(): return (lax.ppermute(block, 'seq', UP), lax.ppermute(block, 'seq', DOWN))  19.6 us
    ppermute x7, starting transfers between devices, ring_far(): far_hi = lax.ppermute(after[1], 'seq', DOWN)  18.8 us
  transfers between devices with their start and end apart: 73, of which 17 were waited for; matrix products, arithmetic and copies ran while one was open for 14% of the time, Pallas kernels for 27%

profile of v1, /device:TPU:1, one launch (start us, length us, event | category | flops | bytes accessed | tf_op | source)
XLA Modules:
  0.0 505.9 jit_solution(15028472863666532538)
XLA Ops:
  85.3 9.1 %collective-permute-start.18 = (bf16[4,4,4,152,128]{4,3,2,1,0:T(8,128)(2,1)S(1)}, bf16[4,4,4,152,128]{4,3,2,1,0:T(8,128)(2,1)}, u32[]{:S(2)}, u32[]{:S(2)}) collective-permute-start(bf16[4,4,4,152,128]{4,3,2,1,0:T(8,128)(2,1)S(1)} %pad_maximum_fusion.1.own_2), channel_id=1, source_target_pairs={{0,8},{8,0},{16,24},{24,16},{32,40},{40,32},{48,56},{56,48},{64,72... | collective-permute-start | bytes 7471112 | tf_op jit(solution)/shard_map/ppermute | solution.py:483
  94.6 4.9 collective-permute-done.11
  117.7 12.2 %shard_map.276 = (bf16[1088,1152]{1,0:T(8,128)(2,1)S(1)}, bf16[1088,2304]{1,0:T(8,128)(2,1)S(1)}, bf16[1088,1088]{1,0:T(8,128)(2,1)S(1)}) custom-call(s32[13]{0:T(128)S(1)} %copy-done.62, bf16[4,4,4,152,128]{4,3,2,1,0:T(8,128)(2,1)} %pad_maximum_fusion.own_1, bf16[4,4,4,152,128]{4,3,2,1,0:T(8,128)(2,1)} %collective-permute-done.13.sib_1, ...), custom_call_target="tpu_custom_call" | custom-call | bytes 31457280 | tf_op jit(solution)/shard_map/pallas_call | solution.py:757
  137.4 13.1 %shard_map.277 = (bf16[1088,4352]{1,0:T(8,128)(2,1)S(1)}, bf16[4352,1088]{1,0:T(8,128)(2,1)S(1)}) custom-call(bf16[2,2,4,4,2,912,128]{6,5,4,3,2,1,0:T(8,128)(2,1)} %bitcast.313, bf16[2,2,4,4,2,912,128]{6,5,4,3,2,1,0:T(8,128)(2,1)} %bitcast.314), custom_call_target="tpu_custom_call" | custom-call | bytes 41943040 | tf_op jit(solution)/shard_map/pallas_call | solution.py:709
  161.8 9.7 %shard_map.278 = (bf16[1088,1152]{1,0:T(8,128)(2,1)S(1)}, bf16[1088,2304]{1,0:T(8,128)(2,1)S(1)}, bf16[1088,1088]{1,0:T(8,128)(2,1)S(1)}) custom-call(bf16[2,2,4,4,2,912,128]{6,5,4,3,2,1,0:T(8,128)(2,1)} %bitcast.315), custom_call_target="tpu_custom_call" | custom-call | bytes 20971520 | tf_op jit(solution)/shard_map/pallas_call | solution.py:709
  184.0 8.1 %shard_map.279 = (bf16[128,1152]{1,0:T(8,128)(2,1)S(1)}, bf16[128,1152]{1,0:T(8,128)(2,1)S(1)}) custom-call(bf16[128,1152]{1,0:T(8,128)(2,1)S(1)} %fusion.5.q_ref, bf16[4,2,64,2304]{3,2,1,0:T(8,128)(2,1)} %pad_maximum_fusion.2.kv_own, bf16[4,2,64,2304]{3,2,1,0:T(8,128)(2,1)} %collective-permute-done.24.kv_sib, s32[128,1]{1,0:T(8,128)S(1)} %copy.151.lpos, ...), custom_call_target="tpu_custom_call" | custom-call | flops 8000000000 | bytes 6291456 | tf_op jit(solution)/shard_map/pallas_call | solution.py:231
  196.5 4.7 copy-done.66
  201.2 5.6 %shard_map.280 = (f32[128,1088]{1,0:T(8,128)S(1)}, bf16[128,1088]{1,0:T(8,128)(2,1)S(1)}, bf16[128,16]{1,0:T(8,128)(2,1)S(1)}, bf16[128,16]{1,0:T(8,128)(2,1)S(1...) custom-call(bf16[128,1152]{1,0:T(8,128)(2,1)S(1)} %get-tuple-element.218.ctx, ...), custom_call_target="tpu_custom_call" | custom-call | flops 10000000000 | bytes 25165824 | tf_op jit(solution)/shard_map/pallas_call | solution.py:425
  213.9 11.7 %all-gather.10.cloned.1.call-done = bf16[1,77824,128]{2,1,0:T(8,128)(2,1)} async-done(((bf16[1,608,128]{2,1,0:T(8,128)(2,1)}), bf16[1,77824,128]{2,1,0:T(8,128)(2,1)}) %all-gather.10.cloned.1.call-update) | async-done | bytes 19922960 | tf_op jit(solution)/shard_map/all_gather | solution.py:801
  225.6 5.6 %collective-permute-done.27 = bf16[2,64,2304]{2,1,0:T(8,128)(2,1)} collective-permute-done((bf16[2,64,2304]{2,1,0:T(8,128)(2,1)S(1)}, bf16[2,64,2304]{2,1,0:T(8,128)(2,1)}, u32[]{:S(2)}, u32[]{:S(2)}) %collective-permute-start.27) | collective-permute-done | bytes 589856 | tf_op jit(solution)/shard_map/ppermute | solution.py:471
  236.1 13.1 %shard_map.281 = (bf16[1088,4352]{1,0:T(8,128)(2,1)S(1)}, bf16[4352,1088]{1,0:T(8,128)(2,1)S(1)}) custom-call(bf16[2,2,4,4,2,608,128]{6,5,4,3,2,1,0:T(8,128)(2,1)} %bitcast.317, bf16[2,2,4,4,2,608,128]{6,5,4,3,2,1,0:T(8,128)(2,1)} %bitcast.318), custom_call_target="tpu_custom_call" | custom-call | bytes 41943040 | tf_op jit(solution)/shard_map/pallas_call | solution.py:709
  256.3 5.8 %shard_map.282 = (bf16[128,1152]{1,0:T(8,128)(2,1)S(1)}, bf16[128,1152]{1,0:T(8,128)(2,1)S(1)}) custom-call(bf16[128,1152]{1,0:T(8,128)(2,1)S(1)} %copy-done.18, bf16[4,2,64,2304]{3,2,1,0:T(8,128)(2,1)S(1)} %pad_maximum_fusion.3.kv_own, bf16[4,2,64,2304]{3,2,1,0:T(8,128)(2,1)S(1)} %collective-permute-done.31.kv_sib, s32[128,1]{1,0:T(8,128)S(1)} %copy-done.38, ...), custom_call_target="tpu_custom_call" | custom-call | flops 8000000000 | bytes 6291456 | tf_op jit(solution)/shard_map/pallas_call | solution.py:231
  265.1 16.4 %shard_map.283 = (bf16[128,1088]{1,0:T(8,128)(2,1)S(1)}, f32[128,1088]{1,0:T(8,128)S(1)}, bf16[128,1152]{1,0:T(8,128)(2,1)S(1)}, bf16[16,1088]{1,0:T(8,128)(2,1)...) custom-call(bf16[128,1152]{1,0:T(8,128)(2,1)S(1)} %get-tuple-element, ...), custom_call_target="tpu_custom_call" | custom-call | flops 17999998976 | bytes 25165824 | tf_op jit(solution)/shard_map/pallas_call | solution.py:425
  295.9 7.1 %shard_map.284.gq = bf16[128,1152]{1,0:T(8,128)(2,1)S(1)} custom-call(bf16[128,1152]{1,0:T(8,128)(2,1)S(1)} %get-tuple-element.242.qe_ref, bf16[128,1152]{1,0:T(8,128)(2,1)S(1)} %get-tuple-element.273.ge_ref, bf16[4,2,64,2304]{3,2,1,0:T(8,128)(2,1)S(1)} %pad_maximum_fusion.3.kv_own, bf16[4,2,64,2304]{3,2,1,0:T(8,128)(2,1)S(1)} %collective-permute-done.31.kv_sib, ...), custom_call_target="tpu_custom_call" | custom-call | flops 8000000000 | bytes 6291456 | tf_op jit(solution)/shard_map/pallas_call | solution.py:231
  316.6 10.5 %shard_map.285 = (bf16[2,64,1152]{2,1,0:T(8,128)(2,1)S(1)}, bf16[2,64,1152]{2,1,0:T(8,128)(2,1)S(1)}) custom-call(bf16[2,64,2304]{2,1,0:T(8,128)(2,1)S(1)} %bitcast.284, bf16[4,2,64,1152]{3,2,1,0:T(8,128)(2,1)} %pad_maximum_fusion.6.q_own, bf16[4,2,64,1152]{3,2,1,0:T(8,128)(2,1)} %collective-permute-done.40.q_sib, ...), custom_call_target="tpu_custom_call" | custom-call | flops 8000000000 | bytes 6291456 | tf_op jit(solution)/shard_map/pallas_call | solution.py:231
  327.1 4.6 shard_map.286
  340.5 17.3 %shard_map.287 = (f32[128,1088]{1,0:T(8,128)}, bf16[128,1152]{1,0:T(8,128)(2,1)}, bf16[16,1088]{1,0:T(8,128)(2,1)}, bf16[16,1088]{1,0:T(8,128)(2,1)}, bf16[16,10...) custom-call(f32[128,1088]{1,0:T(8,128)} %copy-done.74, ...), custom_call_target="tpu_custom_call" | custom-call | flops 16000000000 | bytes 25165824 | tf_op jit(solution)/shard_map/pallas_call | solution.py:425
  362.3 9.6 %shard_map.288.gq = bf16[128,1152]{1,0:T(8,128)(2,1)S(1)} custom-call(bf16[128,1152]{1,0:T(8,128)(2,1)S(1)} %get-tuple-element.217.qe_ref, bf16[128,1152]{1,0:T(8,128)(2,1)S(1)} %copy-done.16, bf16[4,2,64,2304]{3,2,1,0:T(8,128)(2,1)} %pad_maximum_fusion.2.kv_own, bf16[4,2,64,2304]{3,2,1,0:T(8,128)(2,1)} %collective-permute-done.24.kv_sib, ...), custom_call_target="tpu_custom_call" | custom-call | flops 8000000000 | bytes 6291456 | tf_op jit(solution)/shard_map/pallas_call | solution.py:231
  387.9 10.9 %shard_map.289 = (bf16[2,64,1152]{2,1,0:T(8,128)(2,1)S(1)}, bf16[2,64,1152]{2,1,0:T(8,128)(2,1)S(1)}) custom-call(bf16[2,64,2304]{2,1,0:T(8,128)(2,1)S(1)} %bitcast.280, bf16[4,2,64,1152]{3,2,1,0:T(8,128)(2,1)S(1)} %copy-done.9, bf16[4,2,64,1152]{3,2,1,0:T(8,128)(2,1)} %collective-permute-done.50.q_sib, bf16[4,2,64,1152]{3,2,1,0:T(8,128)(2,1)} %pad_maximum_fusion.8.g_own, ...), custom_call_target="tpu_custom_call" | custom-call | flops 8000000000 | bytes 6291456 | tf_op jit(solution)/shard_map/pallas_call | solution.py:231
  404.8 5.4 %all-to-all-start = ((bf16[8,16,2304]{2,1,0:T(8,128)(2,1)}), bf16[8,16,2304]{2,1,0:T(8,128)(2,1)S(1)}, u32[]{:S(2)}, u32[]{:S(2)}) async-start(bf16[8,16,2304]{2,1,0:T(8,128)(2,1)} %maximum_bitcast_fusion.5), calls=%async_computation | async-start | bytes 1179648 | tf_op jit(solution)/shard_map/all_to_all | solution.py:932
  411.8 8.7 %all-to-all-done = bf16[8,16,2304]{2,1,0:T(8,128)(2,1)S(1)} async-done(((bf16[8,16,2304]{2,1,0:T(8,128)(2,1)}), bf16[8,16,2304]{2,1,0:T(8,128)(2,1)S(1)}, u32[]{:S(2)}, u32[]{:S(2)}) %all-to-all-start) | async-done | bytes 589856 | tf_op jit(solution)/shard_map/all_to_all | solution.py:932
  448.6 21.9 %collective-permute-done.61 = bf16[2,1152,128]{2,1,0:T(8,128)(2,1)S(1)} collective-permute-done((bf16[2,1152,128]{2,1,0:T(8,128)(2,1)S(1)}, bf16[2,1152,128]{2,1,0:T(8,128)(2,1)S(1)}, u32[]{:S(2)}, u32[]{:S(2)}) %collective-permute-start.61) | collective-permute-done | bytes 589856 | tf_op jit(solution)/shard_map/ppermute | solution.py:471
  484.0 4.9 collective-permute-start.67
  493.2 5.9 %shard_map.294 = (f32[2,1088,128]{2,1,0:T(8,128)}, f32[2,1088,128]{2,1,0:T(8,128)}, f32[2,1088,128]{2,1,0:T(8,128)}, f32[2,4352,128]{2,1,0:T(8,128)}, f32[2,3264...) custom-call(s32[8]{0:T(128)S(1)} %fusion.44.place, ...), custom_call_target="tpu_custom_call", output_to_operand_aliasing={{0}: (3, {}), {1}: (4, {}), {2}: (5, {}), {3}: (6, {}), {4}... | custom-call | bytes 14680064 | tf_op jit(solution)/shard_map/pallas_call | solution.py:583
  (611 shorter events, 262.1 us)
Async XLA Ops:
  7.2 130.2 %all-gather.8.cloned.1.call-start = ((), (), s32[]{:S(2)}) async-start(), calls=%async_computation.1 | async-start | bytes 30117888 | tf_op jit(solution)/shard_map/all_gather | solution.py:801
  15.1 210.5 %all-gather.10.cloned.1.call-start = ((), (), s32[]{:S(2)}) async-start(), calls=%async_computation.2 | async-start | bytes 20078592 | tf_op jit(solution)/shard_map/all_gather | solution.py:801
  15.8 409.1 %all-gather.12.cloned.1.call-start = ((), (), s32[]{:S(2)}) async-start(), calls=%async_computation.3 | async-start | bytes 2506752 | tf_op jit(solution)/shard_map/all_gather | solution.py:917
  39.2 37.4 %collective-permute-start.19 = (bf16[2,64,1088]{2,1,0:T(8,128)(2,1)}, bf16[2,64,1088]{2,1,0:T(8,128)(2,1)}, u32[]{:S(2)}, u32[]{:S(2)}) collective-permute-start(bf16[2,64,1088]{2,1,0:T(8,128)(2,1)} %pad_maximum_fusion.12), channel_id=1, source_target_pairs={{0,64},{8,72},{16,80},{24,88},{32,96},{40,104},{48,112},{56,120},{... | collective-permute-start | bytes 835592 | tf_op jit(solution)/shard_map/ppermute | solution.py:809
  45.3 33.1 %collective-permute-start.10 = (bf16[4,4,152,128]{3,2,1,0:T(8,128)(2,1)S(1)}, bf16[4,4,152,128]{3,2,1,0:T(8,128)(2,1)}, u32[]{:S(2)}, u32[]{:S(2)}) collective-permute-start(bf16[4,4,152,128]{3,2,1,0:T(8,128)(2,1)S(1)} %pad_maximum_fusion.9), channel_id=1, source_target_pairs={{0,65},{8,73},{2,67},{10,75},{4,69},{12,77},{6,71},{14,79},{16,81}... | collective-permute-start | bytes 1867784 | tf_op jit(solution)/shard_map/ppermute | solution.py:734
  47.9 34.3 %collective-permute-start.9 = (bf16[4,4,152,128]{3,2,1,0:T(8,128)(2,1)S(1)}, bf16[4,4,152,128]{3,2,1,0:T(8,128)(2,1)}, u32[]{:S(2)}, u32[]{:S(2)}) collective-permute-start(bf16[4,4,152,128]{3,2,1,0:T(8,128)(2,1)S(1)} %pad_maximum_fusion.9), channel_id=1, source_target_pairs={{0,1},{8,9},{2,3},{10,11},{4,5},{12,13},{6,7},{14,15},{16,17},{24,... | collective-permute-start | bytes 1867784 | tf_op jit(solution)/shard_map/ppermute | solution.py:733
  47.9 23.0 %collective-permute-start.15 = (bf16[4,4,152,128]{3,2,1,0:T(8,128)(2,1)S(1)}, bf16[4,4,152,128]{3,2,1,0:T(8,128)(2,1)}, u32[]{:S(2)}, u32[]{:S(2)}) collective-permute-start(bf16[4,4,152,128]{3,2,1,0:T(8,128)(2,1)S(1)} %pad_maximum_fusion.10), channel_id=1, source_target_pairs={{0,48},{8,56},{16,0},{24,8},{32,16},{40,24},{48,32},{56,40},{64,11... | collective-permute-start | bytes 1867784 | tf_op jit(solution)/shard_map/ppermute | solution.py:734
  49.6 25.9 %collective-permute-start.14 = (bf16[4,4,152,128]{3,2,1,0:T(8,128)(2,1)S(1)}, bf16[4,4,152,128]{3,2,1,0:T(8,128)(2,1)}, u32[]{:S(2)}, u32[]{:S(2)}) collective-permute-start(bf16[4,4,152,128]{3,2,1,0:T(8,128)(2,1)S(1)} %pad_maximum_fusion.10), channel_id=1, source_target_pairs={{0,16},{8,24},{16,32},{24,40},{32,48},{40,56},{48,0},{56,8},{64,80... | collective-permute-start | bytes 1867784 | tf_op jit(solution)/shard_map/ppermute | solution.py:733
  85.3 27.0 %collective-permute-start.18 = (bf16[4,4,4,152,128]{4,3,2,1,0:T(8,128)(2,1)S(1)}, bf16[4,4,4,152,128]{4,3,2,1,0:T(8,128)(2,1)}, u32[]{:S(2)}, u32[]{:S(2)}) collective-permute-start(bf16[4,4,4,152,128]{4,3,2,1,0:T(8,128)(2,1)S(1)} %pad_maximum_fusion.1.own_2), channel_id=1, source_target_pairs={{0,8},{8,0},{16,24},{24,16},{32,40},{40,32},{48,56},{56,48},{64,72... | collective-permute-start | bytes 7471112 | tf_op jit(solution)/shard_map/ppermute | solution.py:483
  133.6 24.3 %collective-permute-start.20 = (bf16[2,64,2304]{2,1,0:T(8,128)(2,1)S(1)}, bf16[2,64,2304]{2,1,0:T(8,128)(2,1)S(1)}, u32[]{:S(2)}, u32[]{:S(2)}) collective-permute-start(bf16[2,64,2304]{2,1,0:T(8,128)(2,1)S(1)} %bitcast.277), channel_id=1, source_target_pairs={{0,16},{8,24},{16,32},{24,40},{32,48},{40,56},{48,0},{56,8},{64,80... | collective-permute-start | bytes 1769480 | tf_op jit(solution)/shard_map/ppermute | solution.py:471
  133.6 24.3 %collective-permute-start.21 = (bf16[2,64,2304]{2,1,0:T(8,128)(2,1)S(1)}, bf16[2,64,2304]{2,1,0:T(8,128)(2,1)}, u32[]{:S(2)}, u32[]{:S(2)}) collective-permute-start(bf16[2,64,2304]{2,1,0:T(8,128)(2,1)S(1)} %bitcast.278), channel_id=1, source_target_pairs={{0,48},{8,56},{16,0},{24,8},{32,16},{40,24},{48,32},{56,40},{64,11... | collective-permute-start | bytes 1769480 | tf_op jit(solution)/shard_map/ppermute | solution.py:471
  209.6 21.5 %collective-permute-start.27 = (bf16[2,64,2304]{2,1,0:T(8,128)(2,1)S(1)}, bf16[2,64,2304]{2,1,0:T(8,128)(2,1)}, u32[]{:S(2)}, u32[]{:S(2)}) collective-permute-start(bf16[2,64,2304]{2,1,0:T(8,128)(2,1)S(1)} %bitcast.281), channel_id=1, source_target_pairs={{0,16},{8,24},{16,32},{24,40},{32,48},{40,56},{48,0},{56,8},{64,80... | collective-permute-start | bytes 1769480 | tf_op jit(solution)/shard_map/ppermute | solution.py:471
  209.7 21.5 %collective-permute-start.28 = (bf16[2,64,2304]{2,1,0:T(8,128)(2,1)S(1)}, bf16[2,64,2304]{2,1,0:T(8,128)(2,1)}, u32[]{:S(2)}, u32[]{:S(2)}) collective-permute-start(bf16[2,64,2304]{2,1,0:T(8,128)(2,1)S(1)} %bitcast.282), channel_id=1, source_target_pairs={{0,48},{8,56},{16,0},{24,8},{32,16},{40,24},{48,32},{56,40},{64,11... | collective-permute-start | bytes 1769480 | tf_op jit(solution)/shard_map/ppermute | solution.py:471
  252.2 29.4 %collective-permute-start.25 = (bf16[2,64,1152]{2,1,0:T(8,128)(2,1)S(1)}, bf16[2,64,1152]{2,1,0:T(8,128)(2,1)S(1)}, u32[]{:S(2)}, u32[]{:S(2)}) collective-permute-start(bf16[2,64,1152]{2,1,0:T(8,128)(2,1)S(1)} %bitcast.292), channel_id=1, source_target_pairs={{0,16},{8,24},{16,32},{24,40},{32,48},{40,56},{48,0},{56,8},{64,80... | collective-permute-start | bytes 884744 | tf_op jit(solution)/shard_map/ppermute | solution.py:471
  252.3 29.4 %collective-permute-start.26 = (bf16[2,64,1152]{2,1,0:T(8,128)(2,1)S(1)}, bf16[2,64,1152]{2,1,0:T(8,128)(2,1)S(1)}, u32[]{:S(2)}, u32[]{:S(2)}) collective-permute-start(bf16[2,64,1152]{2,1,0:T(8,128)(2,1)S(1)} %bitcast.293), channel_id=1, source_target_pairs={{0,48},{8,56},{16,0},{24,8},{32,16},{40,24},{48,32},{56,40},{64,11... | collective-permute-start | bytes 884744 | tf_op jit(solution)/shard_map/ppermute | solution.py:471
  262.1 19.6 %collective-permute-start.32 = (bf16[2,64,1152]{2,1,0:T(8,128)(2,1)S(1)}, bf16[2,64,1152]{2,1,0:T(8,128)(2,1)S(1)}, u32[]{:S(2)}, u32[]{:S(2)}) collective-permute-start(bf16[2,64,1152]{2,1,0:T(8,128)(2,1)S(1)} %bitcast.298), channel_id=1, source_target_pairs={{0,16},{8,24},{16,32},{24,40},{32,48},{40,56},{48,0},{56,8},{64,80... | collective-permute-start | bytes 884744 | tf_op jit(solution)/shard_map/ppermute | solution.py:471
  336.5 24.2 %collective-permute-start.47 = (bf16[16,2304]{1,0:T(8,128)(2,1)S(1)}, bf16[16,2304]{1,0:T(8,128)(2,1)S(1)}, u32[]{:S(2)}, u32[]{:S(2)}) collective-permute-start(bf16[16,2304]{1,0:T(8,128)(2,1)S(1)} %get-tuple-element.371), channel_id=1, source_target_pairs={{0,32},{8,40},{16,48},{24,56},{32,0},{40,8},{48,16},{56,24},{64,96... | collective-permute-start | bytes 221192 | tf_op jit(solution)/shard_map/ppermute | solution.py:497
  338.6 22.0 %collective-permute-start.46 = (bf16[16,2304]{1,0:T(8,128)(2,1)S(1)}, bf16[16,2304]{1,0:T(8,128)(2,1)S(1)}, u32[]{:S(2)}, u32[]{:S(2)}) collective-permute-start(bf16[16,2304]{1,0:T(8,128)(2,1)S(1)} %get-tuple-element.372), channel_id=1, source_target_pairs={{0,48},{8,56},{16,0},{24,8},{32,16},{40,24},{48,32},{56,40},{64,11... | collective-permute-start | bytes 221192 | tf_op jit(solution)/shard_map/ppermute | solution.py:497
  339.7 21.0 %collective-permute-start.45 = (bf16[16,2304]{1,0:T(8,128)(2,1)S(1)}, bf16[16,2304]{1,0:T(8,128)(2,1)S(1)}, u32[]{:S(2)}, u32[]{:S(2)}) collective-permute-start(bf16[16,2304]{1,0:T(8,128)(2,1)S(1)} %get-tuple-element.370), channel_id=1, source_target_pairs={{0,16},{8,24},{16,32},{24,40},{32,48},{40,56},{48,0},{56,8},{64,80... | collective-permute-start | bytes 221192 | tf_op jit(solution)/shard_map/ppermute | solution.py:497
  410.3 67.5 %all-gather.14.cloned.1.call-start = ((), (), s32[]{:S(2)}) async-start(), calls=%async_computation.4 | async-start | bytes 5308416 | tf_op jit(solution)/shard_map/all_gather | solution.py:938
  442.7 27.8 %collective-permute-start.61 = (bf16[2,1152,128]{2,1,0:T(8,128)(2,1)S(1)}, bf16[2,1152,128]{2,1,0:T(8,128)(2,1)S(1)}, u32[]{:S(2)}, u32[]{:S(2)}) collective-permute-start(bf16[2,1152,128]{2,1,0:T(8,128)(2,1)S(1)} %bitcast.285), channel_id=1, source_target_pairs={{0,16},{8,24},{16,32},{24,40},{32,48},{40,56},{48,0},{56,8},{64,80... | collective-permute-start | bytes 1769480 | tf_op jit(solution)/shard_map/ppermute | solution.py:471
  443.1 30.3 %collective-permute-start.66 = (bf16[64,1088]{1,0:T(8,128)(2,1)S(1)}, bf16[64,1088]{1,0:T(8,128)(2,1)S(1)}, u32[]{:S(2)}, u32[]{:S(2)}) collective-permute-start(bf16[64,1088]{1,0:T(8,128)(2,1)S(1)} %get-tuple-element.390), channel_id=1, source_target_pairs={{0,64},{8,72},{16,80},{24,88},{32,96},{40,104},{48,112},{56,120},{... | collective-permute-start | bytes 417800 | tf_op jit(solution)/shard_map/ppermute | solution.py:943
  444.3 26.4 %collective-permute-start.62 = (bf16[2,1152,128]{2,1,0:T(8,128)(2,1)S(1)}, bf16[2,1152,128]{2,1,0:T(8,128)(2,1)S(1)}, u32[]{:S(2)}, u32[]{:S(2)}) collective-permute-start(bf16[2,1152,128]{2,1,0:T(8,128)(2,1)S(1)} %bitcast.286), channel_id=1, source_target_pairs={{0,48},{8,56},{16,0},{24,8},{32,16},{40,24},{48,32},{56,40},{64,11... | collective-permute-start | bytes 1769480 | tf_op jit(solution)/shard_map/ppermute | solution.py:471
  446.6 27.6 %collective-permute-start.65 = (f32[64,1088]{1,0:T(8,128)S(1)}, f32[64,1088]{1,0:T(8,128)S(1)}, u32[]{:S(2)}, u32[]{:S(2)}) collective-permute-start(f32[64,1088]{1,0:T(8,128)S(1)} %get-tuple-element.369), channel_id=1, source_target_pairs={{0,64},{8,72},{16,80},{24,88},{32,96},{40,104},{48,112},{56,120},{... | collective-permute-start | bytes 835592 | tf_op jit(solution)/shard_map/ppermute | solution.py:943
  (179 other events, 1784.4 us)
Sparse Core Ops, SparseCore 0:
  15.2 119.7 all-gather.7
  138.0 87.5 all-gather.9
  379.2 43.1 all-gather.11
  428.7 46.5 all-gather.13

commit v2 on v1

--- a/solution.py
+++ b/solution.py
@@ -948,8 +948,9 @@
     one = unfold(unfold_late_kernel, 1, one)
     grad_tokens = halves(mine(g.reshape(2, HALF, D)), back_home[0])
     result = halves(mine(result.reshape(2, HALF, D)), back_home[1])
-    own, grad_tokens, result, *one = tie(own, grad_tokens, result, *one)
-    sib = other_core(own).reshape(4, PART, 128)
+    sib = other_core(own)
+    sib, grad_tokens, result, *one = tie(sib, grad_tokens, result, *one)
+    sib = sib.reshape(4, PART, 128)
     ga_q, ga_o, ga_u, ga_d, gb_q, gb_o, gb_d, gb_u = unfold(
         unfold_kernel, 0, place_by_step, own.reshape(4, PART, 128), sib, one
     )

time: 514 us -> 529 us (1.029)
  starting transfers between devices: 123 us -> 129 us
  waiting for transfers between devices: 83.9 us -> 89.9 us
    ppermute x2, waiting for transfers between devices: 0.01 us -> 9.42 us  [shards(): back_home = [lax.ppermute(a, 'seq', SWAP) for a in sent_home]]
    ppermute x9, starting transfers between devices: 31.9 us -> 38.4 us  [other_core(): return lax.ppermute(own, 'seq', CORE)]
    another operation x14 -> x15, other arithmetic: 12.9 us -> 16.7 us  [ring_far(): own = jnp.stack([block, before, after, jnp.stack([far_lo, far_hi])])]
    unnamed x266 -> x262, local copies, waits for them, and re-layouts: 32.1 us -> 30.6 us
  transfers between devices with their start and end apart: 73 -> 73, of which waited for: 17 -> 19; matrix products, arithmetic and copies ran while one was open for 14% -> 15% of each run, Pallas kernels for 27% -> 27%
where the time goes in v2:
time: 529 us; the launch traced here: 519 us
  Pallas kernels  161 us (30%)
  starting transfers between devices  129 us (24%)
  waiting for transfers between devices  89.9 us (17%)
  local copies, waits for them, and re-layouts  76.2 us (14%)
  other arithmetic  39.8 us (8%)
  between operations  17 us (3%)
    pallas_call x6, Pallas kernels, attention_call(): pl.pallas_call(kernel, out_shape=outs, in_specs=[HERE] * len(args), out_s...  52 us
    pallas_call x3, Pallas kernels, mlp_call(): pl.pallas_call(kernel, out_shape=outs, in_specs=[HERE] * (len(args) - wei...  39.4 us
    ppermute x9, starting transfers between devices, other_core(): return lax.ppermute(own, 'seq', CORE)  38.4 us
    pallas_call x3, Pallas kernels, unpack(): pl.pallas_call(kernel, grid=(8,), out_shape=tuple((jax.ShapeDtypeStruct((...  35.9 us
    unnamed x262, local copies, waits for them, and re-layouts  30.6 us
    ppermute x14, waiting for transfers between devices, ring_start(): return (lax.ppermute(block, 'seq', UP), lax.ppermute(block, 'seq', DOWN))  29.1 us
    ppermute x14, starting transfers between devices, ring_start(): return (lax.ppermute(block, 'seq', UP), lax.ppermute(block, 'seq', DOWN))  19.4 us
    ppermute x7, starting transfers between devices, ring_far(): far_hi = lax.ppermute(after[1], 'seq', DOWN)  18.4 us
  transfers between devices with their start and end apart: 73, of which 19 were waited for; matrix products, arithmetic and copies ran while one was open for 15% of the time, Pallas kernels for 27%

profile of v2, /device:TPU:1, one launch (start us, length us, event | category | flops | bytes accessed | tf_op | source)
XLA Modules:
  0.0 518.7 jit_solution(8662331553449215922)
XLA Ops:
  81.5 8.5 %collective-permute-start.18 = (bf16[4,4,4,152,128]{4,3,2,1,0:T(8,128)(2,1)S(1)}, bf16[4,4,4,152,128]{4,3,2,1,0:T(8,128)(2,1)}, u32[]{:S(2)}, u32[]{:S(2)}) collective-permute-start(bf16[4,4,4,152,128]{4,3,2,1,0:T(8,128)(2,1)S(1)} %pad_maximum_fusion.1.own_2), channel_id=1, source_target_pairs={{0,8},{8,0},{16,24},{24,16},{32,40},{40,32},{48,56},{56,48},{64,72... | collective-permute-start | bytes 7471112 | tf_op jit(solution)/shard_map/ppermute | solution.py:483
  93.5 10.3 %collective-permute-start.13 = (bf16[4,4,4,152,128]{4,3,2,1,0:T(8,128)(2,1)}, bf16[4,4,4,152,128]{4,3,2,1,0:T(8,128)(2,1)}, u32[]{:S(2)}, u32[]{:S(2)}) collective-permute-start(bf16[4,4,4,152,128]{4,3,2,1,0:T(8,128)(2,1)} %pad_maximum_fusion.own_1), channel_id=1, source_target_pairs={{0,8},{8,0},{16,24},{24,16},{32,40},{40,32},{48,56},{56,48},{64,72... | collective-permute-start | bytes 7471112 | tf_op jit(solution)/shard_map/ppermute | solution.py:483
  114.4 12.1 %shard_map.276 = (bf16[1088,1152]{1,0:T(8,128)(2,1)S(1)}, bf16[1088,2304]{1,0:T(8,128)(2,1)S(1)}, bf16[1088,1088]{1,0:T(8,128)(2,1)S(1)}) custom-call(s32[13]{0:T(128)S(1)} %copy-done.62, bf16[4,4,4,152,128]{4,3,2,1,0:T(8,128)(2,1)} %pad_maximum_fusion.own_1, bf16[4,4,4,152,128]{4,3,2,1,0:T(8,128)(2,1)} %collective-permute-done.13.sib_1, ...), custom_call_target="tpu_custom_call" | custom-call | bytes 31457280 | tf_op jit(solution)/shard_map/pallas_call | solution.py:757
  133.8 13.1 %shard_map.277 = (bf16[1088,4352]{1,0:T(8,128)(2,1)S(1)}, bf16[4352,1088]{1,0:T(8,128)(2,1)S(1)}) custom-call(bf16[2,2,4,4,2,912,128]{6,5,4,3,2,1,0:T(8,128)(2,1)} %bitcast.316, bf16[2,2,4,4,2,912,128]{6,5,4,3,2,1,0:T(8,128)(2,1)} %bitcast.317), custom_call_target="tpu_custom_call" | custom-call | bytes 41943040 | tf_op jit(solution)/shard_map/pallas_call | solution.py:709
  158.2 9.7 %shard_map.278 = (bf16[1088,1152]{1,0:T(8,128)(2,1)S(1)}, bf16[1088,2304]{1,0:T(8,128)(2,1)S(1)}, bf16[1088,1088]{1,0:T(8,128)(2,1)S(1)}) custom-call(bf16[2,2,4,4,2,912,128]{6,5,4,3,2,1,0:T(8,128)(2,1)} %bitcast.318), custom_call_target="tpu_custom_call" | custom-call | bytes 20971520 | tf_op jit(solution)/shard_map/pallas_call | solution.py:709
  181.2 8.1 %shard_map.279 = (bf16[128,1152]{1,0:T(8,128)(2,1)S(1)}, bf16[128,1152]{1,0:T(8,128)(2,1)S(1)}) custom-call(bf16[128,1152]{1,0:T(8,128)(2,1)S(1)} %fusion.5.q_ref, bf16[4,2,64,2304]{3,2,1,0:T(8,128)(2,1)} %pad_maximum_fusion.2.kv_own, bf16[4,2,64,2304]{3,2,1,0:T(8,128)(2,1)} %collective-permute-done.24.kv_sib, s32[128,1]{1,0:T(8,128)S(1)} %copy.151.lpos, ...), custom_call_target="tpu_custom_call" | custom-call | flops 8000000000 | bytes 6291456 | tf_op jit(solution)/shard_map/pallas_call | solution.py:231
  193.4 4.7 copy-done.66
  198.1 5.6 %shard_map.280 = (f32[128,1088]{1,0:T(8,128)S(1)}, bf16[128,1088]{1,0:T(8,128)(2,1)S(1)}, bf16[128,16]{1,0:T(8,128)(2,1)S(1)}, bf16[128,16]{1,0:T(8,128)(2,1)S(1...) custom-call(bf16[128,1152]{1,0:T(8,128)(2,1)S(1)} %get-tuple-element.218.ctx, ...), custom_call_target="tpu_custom_call" | custom-call | flops 10000000000 | bytes 25165824 | tf_op jit(solution)/shard_map/pallas_call | solution.py:425
  210.8 14.7 %all-gather.10.cloned.1.call-done = bf16[1,77824,128]{2,1,0:T(8,128)(2,1)} async-done(((bf16[1,608,128]{2,1,0:T(8,128)(2,1)}), bf16[1,77824,128]{2,1,0:T(8,128)(2,1)}) %all-gather.10.cloned.1.call-update) | async-done | bytes 19922960 | tf_op jit(solution)/shard_map/all_gather | solution.py:801
  234.5 13.1 %shard_map.281 = (bf16[1088,4352]{1,0:T(8,128)(2,1)S(1)}, bf16[4352,1088]{1,0:T(8,128)(2,1)S(1)}) custom-call(bf16[2,2,4,4,2,608,128]{6,5,4,3,2,1,0:T(8,128)(2,1)} %bitcast.320, bf16[2,2,4,4,2,608,128]{6,5,4,3,2,1,0:T(8,128)(2,1)} %bitcast.321), custom_call_target="tpu_custom_call" | custom-call | bytes 41943040 | tf_op jit(solution)/shard_map/pallas_call | solution.py:709
  254.7 5.8 %shard_map.282 = (bf16[128,1152]{1,0:T(8,128)(2,1)S(1)}, bf16[128,1152]{1,0:T(8,128)(2,1)S(1)}) custom-call(bf16[128,1152]{1,0:T(8,128)(2,1)S(1)} %copy-done.18, bf16[4,2,64,2304]{3,2,1,0:T(8,128)(2,1)S(1)} %pad_maximum_fusion.3.kv_own, bf16[4,2,64,2304]{3,2,1,0:T(8,128)(2,1)S(1)} %collective-permute-done.31.kv_sib, s32[128,1]{1,0:T(8,128)S(1)} %copy-done.38, ...), custom_call_target="tpu_custom_call" | custom-call | flops 8000000000 | bytes 6291456 | tf_op jit(solution)/shard_map/pallas_call | solution.py:231
  263.5 16.4 %shard_map.283 = (bf16[128,1088]{1,0:T(8,128)(2,1)S(1)}, f32[128,1088]{1,0:T(8,128)S(1)}, bf16[128,1152]{1,0:T(8,128)(2,1)S(1)}, bf16[16,1088]{1,0:T(8,128)(2,1)...) custom-call(bf16[128,1152]{1,0:T(8,128)(2,1)S(1)} %get-tuple-element, ...), custom_call_target="tpu_custom_call" | custom-call | flops 17999998976 | bytes 25165824 | tf_op jit(solution)/shard_map/pallas_call | solution.py:425
  294.3 7.1 %shard_map.284.gq = bf16[128,1152]{1,0:T(8,128)(2,1)S(1)} custom-call(bf16[128,1152]{1,0:T(8,128)(2,1)S(1)} %get-tuple-element.242.qe_ref, bf16[128,1152]{1,0:T(8,128)(2,1)S(1)} %get-tuple-element.273.ge_ref, bf16[4,2,64,2304]{3,2,1,0:T(8,128)(2,1)S(1)} %pad_maximum_fusion.3.kv_own, bf16[4,2,64,2304]{3,2,1,0:T(8,128)(2,1)S(1)} %collective-permute-done.31.kv_sib, ...), custom_call_target="tpu_custom_call" | custom-call | flops 8000000000 | bytes 6291456 | tf_op jit(solution)/shard_map/pallas_call | solution.py:231
  315.0 10.5 %shard_map.285 = (bf16[2,64,1152]{2,1,0:T(8,128)(2,1)S(1)}, bf16[2,64,1152]{2,1,0:T(8,128)(2,1)S(1)}) custom-call(bf16[2,64,2304]{2,1,0:T(8,128)(2,1)S(1)} %bitcast.290, bf16[4,2,64,1152]{3,2,1,0:T(8,128)(2,1)} %pad_maximum_fusion.7.q_own, bf16[4,2,64,1152]{3,2,1,0:T(8,128)(2,1)} %collective-permute-done.40.q_sib, ...), custom_call_target="tpu_custom_call" | custom-call | flops 8000000000 | bytes 6291456 | tf_op jit(solution)/shard_map/pallas_call | solution.py:231
  325.6 4.6 shard_map.286
  339.0 17.3 %shard_map.287 = (f32[128,1088]{1,0:T(8,128)}, bf16[128,1152]{1,0:T(8,128)(2,1)}, bf16[16,1088]{1,0:T(8,128)(2,1)}, bf16[16,1088]{1,0:T(8,128)(2,1)}, bf16[16,10...) custom-call(f32[128,1088]{1,0:T(8,128)} %copy-done.74, ...), custom_call_target="tpu_custom_call" | custom-call | flops 16000000000 | bytes 25165824 | tf_op jit(solution)/shard_map/pallas_call | solution.py:425
  360.8 9.6 %shard_map.288.gq = bf16[128,1152]{1,0:T(8,128)(2,1)S(1)} custom-call(bf16[128,1152]{1,0:T(8,128)(2,1)S(1)} %get-tuple-element.217.qe_ref, bf16[128,1152]{1,0:T(8,128)(2,1)S(1)} %copy-done.16, bf16[4,2,64,2304]{3,2,1,0:T(8,128)(2,1)} %pad_maximum_fusion.2.kv_own, bf16[4,2,64,2304]{3,2,1,0:T(8,128)(2,1)} %collective-permute-done.24.kv_sib, ...), custom_call_target="tpu_custom_call" | custom-call | flops 8000000000 | bytes 6291456 | tf_op jit(solution)/shard_map/pallas_call | solution.py:231
  386.4 10.9 %shard_map.289 = (bf16[2,64,1152]{2,1,0:T(8,128)(2,1)S(1)}, bf16[2,64,1152]{2,1,0:T(8,128)(2,1)S(1)}) custom-call(bf16[2,64,2304]{2,1,0:T(8,128)(2,1)S(1)} %bitcast.286, bf16[4,2,64,1152]{3,2,1,0:T(8,128)(2,1)S(1)} %copy-done.9, bf16[4,2,64,1152]{3,2,1,0:T(8,128)(2,1)} %collective-permute-done.50.q_sib, bf16[4,2,64,1152]{3,2,1,0:T(8,128)(2,1)} %pad_maximum_fusion.9.g_own, ...), custom_call_target="tpu_custom_call" | custom-call | flops 8000000000 | bytes 6291456 | tf_op jit(solution)/shard_map/pallas_call | solution.py:231
  403.3 5.4 %all-to-all-start = ((bf16[8,16,2304]{2,1,0:T(8,128)(2,1)}), bf16[8,16,2304]{2,1,0:T(8,128)(2,1)S(1)}, u32[]{:S(2)}, u32[]{:S(2)}) async-start(bf16[8,16,2304]{2,1,0:T(8,128)(2,1)} %maximum_bitcast_fusion.5), calls=%async_computation | async-start | bytes 1179648 | tf_op jit(solution)/shard_map/all_to_all | solution.py:932
  410.2 8.7 %all-to-all-done = bf16[8,16,2304]{2,1,0:T(8,128)(2,1)S(1)} async-done(((bf16[8,16,2304]{2,1,0:T(8,128)(2,1)}), bf16[8,16,2304]{2,1,0:T(8,128)(2,1)S(1)}, u32[]{:S(2)}, u32[]{:S(2)}) %all-to-all-start) | async-done | bytes 589856 | tf_op jit(solution)/shard_map/all_to_all | solution.py:932
  443.8 25.1 %collective-permute-done.61 = bf16[2,1152,128]{2,1,0:T(8,128)(2,1)S(1)} collective-permute-done((bf16[2,1152,128]{2,1,0:T(8,128)(2,1)S(1)}, bf16[2,1152,128]{2,1,0:T(8,128)(2,1)S(1)}, u32[]{:S(2)}, u32[]{:S(2)}) %collective-permute-start.61) | collective-permute-done | bytes 589856 | tf_op jit(solution)/shard_map/ppermute | solution.py:471
  478.4 4.9 collective-permute-start.65
  491.9 5.5 %collective-permute-done.66 = f32[64,1088]{1,0:T(8,128)S(1)} collective-permute-done((f32[64,1088]{1,0:T(8,128)S(1)}, f32[64,1088]{1,0:T(8,128)S(1)}, u32[]{:S(2)}, u32[]{:S(2)}) %collective-permute-start.66) | collective-permute-done | bytes 278560 | tf_op jit(solution)/shard_map/ppermute | solution.py:943
  506.0 5.9 %shard_map.294 = (f32[2,1088,128]{2,1,0:T(8,128)}, f32[2,1088,128]{2,1,0:T(8,128)}, f32[2,1088,128]{2,1,0:T(8,128)}, f32[2,4352,128]{2,1,0:T(8,128)}, f32[2,3264...) custom-call(s32[8]{0:T(128)S(1)} %fusion.44.place, ...), custom_call_target="tpu_custom_call", output_to_operand_aliasing={{0}: (3, {}), {1}: (4, {}), {2}: (5, {}), {3}: (6, {}), {4}... | custom-call | bytes 14680064 | tf_op jit(solution)/shard_map/pallas_call | solution.py:583
  (608 shorter events, 264.0 us)
Async XLA Ops:
  7.2 126.6 %all-gather.8.cloned.1.call-start = ((), (), s32[]{:S(2)}) async-start(), calls=%async_computation.1 | async-start | bytes 30117888 | tf_op jit(solution)/shard_map/all_gather | solution.py:801
  15.1 210.4 %all-gather.10.cloned.1.call-start = ((), (), s32[]{:S(2)}) async-start(), calls=%async_computation.2 | async-start | bytes 20078592 | tf_op jit(solution)/shard_map/all_gather | solution.py:801
  15.9 407.5 %all-gather.12.cloned.1.call-start = ((), (), s32[]{:S(2)}) async-start(), calls=%async_computation.3 | async-start | bytes 2506752 | tf_op jit(solution)/shard_map/all_gather | solution.py:917
  39.3 33.5 %collective-permute-start.19 = (bf16[2,64,1088]{2,1,0:T(8,128)(2,1)}, bf16[2,64,1088]{2,1,0:T(8,128)(2,1)}, u32[]{:S(2)}, u32[]{:S(2)}) collective-permute-start(bf16[2,64,1088]{2,1,0:T(8,128)(2,1)} %pad_maximum_fusion.14), channel_id=1, source_target_pairs={{0,64},{8,72},{16,80},{24,88},{32,96},{40,104},{48,112},{56,120},{... | collective-permute-start | bytes 835592 | tf_op jit(solution)/shard_map/ppermute | solution.py:809
  43.7 31.0 %collective-permute-start.10 = (bf16[4,4,152,128]{3,2,1,0:T(8,128)(2,1)S(1)}, bf16[4,4,152,128]{3,2,1,0:T(8,128)(2,1)}, u32[]{:S(2)}, u32[]{:S(2)}) collective-permute-start(bf16[4,4,152,128]{3,2,1,0:T(8,128)(2,1)S(1)} %pad_maximum_fusion.10), channel_id=1, source_target_pairs={{0,65},{8,73},{2,67},{10,75},{4,69},{12,77},{6,71},{14,79},{16,81}... | collective-permute-start | bytes 1867784 | tf_op jit(solution)/shard_map/ppermute | solution.py:734
  46.2 31.7 %collective-permute-start.9 = (bf16[4,4,152,128]{3,2,1,0:T(8,128)(2,1)S(1)}, bf16[4,4,152,128]{3,2,1,0:T(8,128)(2,1)}, u32[]{:S(2)}, u32[]{:S(2)}) collective-permute-start(bf16[4,4,152,128]{3,2,1,0:T(8,128)(2,1)S(1)} %pad_maximum_fusion.10), channel_id=1, source_target_pairs={{0,1},{8,9},{2,3},{10,11},{4,5},{12,13},{6,7},{14,15},{16,17},{24,... | collective-permute-start | bytes 1867784 | tf_op jit(solution)/shard_map/ppermute | solution.py:733
  46.2 20.8 %collective-permute-start.15 = (bf16[4,4,152,128]{3,2,1,0:T(8,128)(2,1)S(1)}, bf16[4,4,152,128]{3,2,1,0:T(8,128)(2,1)}, u32[]{:S(2)}, u32[]{:S(2)}) collective-permute-start(bf16[4,4,152,128]{3,2,1,0:T(8,128)(2,1)S(1)} %pad_maximum_fusion.11), channel_id=1, source_target_pairs={{0,48},{8,56},{16,0},{24,8},{32,16},{40,24},{48,32},{56,40},{64,11... | collective-permute-start | bytes 1867784 | tf_op jit(solution)/shard_map/ppermute | solution.py:734
  48.0 23.8 %collective-permute-start.14 = (bf16[4,4,152,128]{3,2,1,0:T(8,128)(2,1)S(1)}, bf16[4,4,152,128]{3,2,1,0:T(8,128)(2,1)}, u32[]{:S(2)}, u32[]{:S(2)}) collective-permute-start(bf16[4,4,152,128]{3,2,1,0:T(8,128)(2,1)S(1)} %pad_maximum_fusion.11), channel_id=1, source_target_pairs={{0,16},{8,24},{16,32},{24,40},{32,48},{40,56},{48,0},{56,8},{64,80... | collective-permute-start | bytes 1867784 | tf_op jit(solution)/shard_map/ppermute | solution.py:733
  81.5 27.6 %collective-permute-start.18 = (bf16[4,4,4,152,128]{4,3,2,1,0:T(8,128)(2,1)S(1)}, bf16[4,4,4,152,128]{4,3,2,1,0:T(8,128)(2,1)}, u32[]{:S(2)}, u32[]{:S(2)}) collective-permute-start(bf16[4,4,4,152,128]{4,3,2,1,0:T(8,128)(2,1)S(1)} %pad_maximum_fusion.1.own_2), channel_id=1, source_target_pairs={{0,8},{8,0},{16,24},{24,16},{32,40},{40,32},{48,56},{56,48},{64,72... | collective-permute-start | bytes 7471112 | tf_op jit(solution)/shard_map/ppermute | solution.py:483
  93.5 20.3 %collective-permute-start.13 = (bf16[4,4,4,152,128]{4,3,2,1,0:T(8,128)(2,1)}, bf16[4,4,4,152,128]{4,3,2,1,0:T(8,128)(2,1)}, u32[]{:S(2)}, u32[]{:S(2)}) collective-permute-start(bf16[4,4,4,152,128]{4,3,2,1,0:T(8,128)(2,1)} %pad_maximum_fusion.own_1), channel_id=1, source_target_pairs={{0,8},{8,0},{16,24},{24,16},{32,40},{40,32},{48,56},{56,48},{64,72... | collective-permute-start | bytes 7471112 | tf_op jit(solution)/shard_map/ppermute | solution.py:483
  130.3 24.1 %collective-permute-start.20 = (bf16[2,64,2304]{2,1,0:T(8,128)(2,1)S(1)}, bf16[2,64,2304]{2,1,0:T(8,128)(2,1)S(1)}, u32[]{:S(2)}, u32[]{:S(2)}) collective-permute-start(bf16[2,64,2304]{2,1,0:T(8,128)(2,1)S(1)} %bitcast.283), channel_id=1, source_target_pairs={{0,16},{8,24},{16,32},{24,40},{32,48},{40,56},{48,0},{56,8},{64,80... | collective-permute-start | bytes 1769480 | tf_op jit(solution)/shard_map/ppermute | solution.py:471
  131.7 22.7 %collective-permute-start.21 = (bf16[2,64,2304]{2,1,0:T(8,128)(2,1)S(1)}, bf16[2,64,2304]{2,1,0:T(8,128)(2,1)}, u32[]{:S(2)}, u32[]{:S(2)}) collective-permute-start(bf16[2,64,2304]{2,1,0:T(8,128)(2,1)S(1)} %bitcast.284), channel_id=1, source_target_pairs={{0,48},{8,56},{16,0},{24,8},{32,16},{40,24},{48,32},{56,40},{64,11... | collective-permute-start | bytes 1769480 | tf_op jit(solution)/shard_map/ppermute | solution.py:471
  206.5 23.0 %collective-permute-start.27 = (bf16[2,64,2304]{2,1,0:T(8,128)(2,1)S(1)}, bf16[2,64,2304]{2,1,0:T(8,128)(2,1)}, u32[]{:S(2)}, u32[]{:S(2)}) collective-permute-start(bf16[2,64,2304]{2,1,0:T(8,128)(2,1)S(1)} %bitcast.287), channel_id=1, source_target_pairs={{0,16},{8,24},{16,32},{24,40},{32,48},{40,56},{48,0},{56,8},{64,80... | collective-permute-start | bytes 1769480 | tf_op jit(solution)/shard_map/ppermute | solution.py:471
  206.6 22.9 %collective-permute-start.28 = (bf16[2,64,2304]{2,1,0:T(8,128)(2,1)S(1)}, bf16[2,64,2304]{2,1,0:T(8,128)(2,1)}, u32[]{:S(2)}, u32[]{:S(2)}) collective-permute-start(bf16[2,64,2304]{2,1,0:T(8,128)(2,1)S(1)} %bitcast.288), channel_id=1, source_target_pairs={{0,48},{8,56},{16,0},{24,8},{32,16},{40,24},{48,32},{56,40},{64,11... | collective-permute-start | bytes 1769480 | tf_op jit(solution)/shard_map/ppermute | solution.py:471
  250.6 29.4 %collective-permute-start.25 = (bf16[2,64,1152]{2,1,0:T(8,128)(2,1)S(1)}, bf16[2,64,1152]{2,1,0:T(8,128)(2,1)S(1)}, u32[]{:S(2)}, u32[]{:S(2)}) collective-permute-start(bf16[2,64,1152]{2,1,0:T(8,128)(2,1)S(1)} %bitcast.295), channel_id=1, source_target_pairs={{0,16},{8,24},{16,32},{24,40},{32,48},{40,56},{48,0},{56,8},{64,80... | collective-permute-start | bytes 884744 | tf_op jit(solution)/shard_map/ppermute | solution.py:471
  250.7 29.4 %collective-permute-start.26 = (bf16[2,64,1152]{2,1,0:T(8,128)(2,1)S(1)}, bf16[2,64,1152]{2,1,0:T(8,128)(2,1)S(1)}, u32[]{:S(2)}, u32[]{:S(2)}) collective-permute-start(bf16[2,64,1152]{2,1,0:T(8,128)(2,1)S(1)} %bitcast.296), channel_id=1, source_target_pairs={{0,48},{8,56},{16,0},{24,8},{32,16},{40,24},{48,32},{56,40},{64,11... | collective-permute-start | bytes 884744 | tf_op jit(solution)/shard_map/ppermute | solution.py:471
  260.5 19.6 %collective-permute-start.32 = (bf16[2,64,1152]{2,1,0:T(8,128)(2,1)S(1)}, bf16[2,64,1152]{2,1,0:T(8,128)(2,1)S(1)}, u32[]{:S(2)}, u32[]{:S(2)}) collective-permute-start(bf16[2,64,1152]{2,1,0:T(8,128)(2,1)S(1)} %bitcast.301), channel_id=1, source_target_pairs={{0,16},{8,24},{16,32},{24,40},{32,48},{40,56},{48,0},{56,8},{64,80... | collective-permute-start | bytes 884744 | tf_op jit(solution)/shard_map/ppermute | solution.py:471
  334.9 24.2 %collective-permute-start.47 = (bf16[16,2304]{1,0:T(8,128)(2,1)S(1)}, bf16[16,2304]{1,0:T(8,128)(2,1)S(1)}, u32[]{:S(2)}, u32[]{:S(2)}) collective-permute-start(bf16[16,2304]{1,0:T(8,128)(2,1)S(1)} %get-tuple-element.373), channel_id=1, source_target_pairs={{0,32},{8,40},{16,48},{24,56},{32,0},{40,8},{48,16},{56,24},{64,96... | collective-permute-start | bytes 221192 | tf_op jit(solution)/shard_map/ppermute | solution.py:497
  337.1 22.0 %collective-permute-start.46 = (bf16[16,2304]{1,0:T(8,128)(2,1)S(1)}, bf16[16,2304]{1,0:T(8,128)(2,1)S(1)}, u32[]{:S(2)}, u32[]{:S(2)}) collective-permute-start(bf16[16,2304]{1,0:T(8,128)(2,1)S(1)} %get-tuple-element.374), channel_id=1, source_target_pairs={{0,48},{8,56},{16,0},{24,8},{32,16},{40,24},{48,32},{56,40},{64,11... | collective-permute-start | bytes 221192 | tf_op jit(solution)/shard_map/ppermute | solution.py:497
  338.1 21.0 %collective-permute-start.45 = (bf16[16,2304]{1,0:T(8,128)(2,1)S(1)}, bf16[16,2304]{1,0:T(8,128)(2,1)S(1)}, u32[]{:S(2)}, u32[]{:S(2)}) collective-permute-start(bf16[16,2304]{1,0:T(8,128)(2,1)S(1)} %get-tuple-element.372), channel_id=1, source_target_pairs={{0,16},{8,24},{16,32},{24,40},{32,48},{40,56},{48,0},{56,8},{64,80... | collective-permute-start | bytes 221192 | tf_op jit(solution)/shard_map/ppermute | solution.py:497
  408.7 91.0 %all-gather.14.cloned.1.call-start = ((), (), s32[]{:S(2)}) async-start(), calls=%async_computation.4 | async-start | bytes 5308416 | tf_op jit(solution)/shard_map/all_gather | solution.py:938
  441.1 27.8 %collective-permute-start.61 = (bf16[2,1152,128]{2,1,0:T(8,128)(2,1)S(1)}, bf16[2,1152,128]{2,1,0:T(8,128)(2,1)S(1)}, u32[]{:S(2)}, u32[]{:S(2)}) collective-permute-start(bf16[2,1152,128]{2,1,0:T(8,128)(2,1)S(1)} %bitcast.272), channel_id=1, source_target_pairs={{0,16},{8,24},{16,32},{24,40},{32,48},{40,56},{48,0},{56,8},{64,80... | collective-permute-start | bytes 1769480 | tf_op jit(solution)/shard_map/ppermute | solution.py:471
  441.4 27.6 %collective-permute-start.62 = (bf16[2,1152,128]{2,1,0:T(8,128)(2,1)S(1)}, bf16[2,1152,128]{2,1,0:T(8,128)(2,1)S(1)}, u32[]{:S(2)}, u32[]{:S(2)}) collective-permute-start(bf16[2,1152,128]{2,1,0:T(8,128)(2,1)S(1)} %bitcast.273), channel_id=1, source_target_pairs={{0,48},{8,56},{16,0},{24,8},{32,16},{40,24},{48,32},{56,40},{64,11... | collective-permute-start | bytes 1769480 | tf_op jit(solution)/shard_map/ppermute | solution.py:471
  478.4 27.6 %collective-permute-start.65 = (bf16[4,2,1152,128]{3,2,1,0:T(8,128)(2,1)}, bf16[4,2,1152,128]{3,2,1,0:T(8,128)(2,1)}, u32[]{:S(2)}, u32[]{:S(2)}) collective-permute-start(bf16[4,2,1152,128]{3,2,1,0:T(8,128)(2,1)} %pad_maximum_fusion.4), channel_id=1, source_target_pairs={{0,8},{8,0},{16,24},{24,16},{32,40},{40,32},{48,56},{56,48},{64,72... | collective-permute-start | bytes 7077896 | tf_op jit(solution)/shard_map/ppermute | solution.py:483
  (177 other events, 1756.6 us)
Sparse Core Ops, SparseCore 0:
  15.2 117.2 all-gather.7
  135.5 89.9 all-gather.9
  377.6 43.1 all-gather.11
  427.1 46.5 all-gather.13

commit v3 on v2

--- a/solution.py
+++ b/solution.py
@@ -948,8 +948,9 @@
     one = unfold(unfold_late_kernel, 1, one)
     grad_tokens = halves(mine(g.reshape(2, HALF, D)), back_home[0])
     result = halves(mine(result.reshape(2, HALF, D)), back_home[1])
+    own, grad_tokens, result = tie(own, grad_tokens, result)
     sib = other_core(own)
-    sib, grad_tokens, result, *one = tie(sib, grad_tokens, result, *one)
+    sib, *one = tie(sib, *one)
     sib = sib.reshape(4, PART, 128)
     ga_q, ga_o, ga_u, ga_d, gb_q, gb_o, gb_d, gb_u = unfold(
         unfold_kernel, 0, place_by_step, own.reshape(4, PART, 128), sib, one

time: 529 us -> 510 us (0.964)
  waiting for transfers between devices: 89.9 us -> 80.4 us
  starting transfers between devices: 129 us -> 123 us
    ppermute x2, waiting for transfers between devices: 9.42 us -> 0.01 us  [shards(): back_home = [lax.ppermute(a, 'seq', SWAP) for a in sent_home]]
    ppermute x9, starting transfers between devices: 38.4 us -> 32.2 us  [other_core(): return lax.ppermute(own, 'seq', CORE)]
    another operation x15 -> x14, other arithmetic: 16.7 us -> 13 us  [ring_far(): own = jnp.stack([block, before, after, jnp.stack([far_lo, far_hi])])]
    unnamed x262 -> x266, local copies, waits for them, and re-layouts: 30.6 us -> 32.2 us
  transfers between devices with their start and end apart: 73 -> 73, of which waited for: 19 -> 17; matrix products, arithmetic and copies ran while one was open for 15% -> 15% of each run, Pallas kernels for 27% -> 28%
where the time goes in v3:
time: 510 us; the launch traced here: 502 us
  Pallas kernels  162 us (32%)
  starting transfers between devices  123 us (24%)
  waiting for transfers between devices  80.4 us (16%)
  local copies, waits for them, and re-layouts  76.7 us (15%)
  other arithmetic  38.5 us (8%)
  between operations  17 us (3%)
  matrix products  5.27 us (1%)
    pallas_call x6, Pallas kernels, attention_call(): pl.pallas_call(kernel, out_shape=outs, in_specs=[HERE] * len(args), out_s...  52 us
    pallas_call x3, Pallas kernels, mlp_call(): pl.pallas_call(kernel, out_shape=outs, in_specs=[HERE] * (len(args) - wei...  39.4 us
    pallas_call x3, Pallas kernels, unpack(): pl.pallas_call(kernel, grid=(8,), out_shape=tuple((jax.ShapeDtypeStruct((...  35.9 us
    unnamed x266, local copies, waits for them, and re-layouts  32.2 us
    ppermute x9, starting transfers between devices, other_core(): return lax.ppermute(own, 'seq', CORE)  32.2 us
    ppermute x14, waiting for transfers between devices, ring_start(): return (lax.ppermute(block, 'seq', UP), lax.ppermute(block, 'seq', DOWN))  27.7 us
    ppermute x14, starting transfers between devices, ring_start(): return (lax.ppermute(block, 'seq', UP), lax.ppermute(block, 'seq', DOWN))  19.6 us
    ppermute x7, starting transfers between devices, ring_far(): far_hi = lax.ppermute(after[1], 'seq', DOWN)  18.6 us
  transfers between devices with their start and end apart: 73, of which 17 were waited for; matrix products, arithmetic and copies ran while one was open for 15% of the time, Pallas kernels for 28%

profile of v3, /device:TPU:1, one launch (start us, length us, event | category | flops | bytes accessed | tf_op | source)
XLA Modules:
  0.0 502.4 jit_solution(8523652184749716522)
XLA Ops:
  67.0 4.7 collective-permute-done.15
  86.1 9.0 %collective-permute-start.18 = (bf16[4,4,4,152,128]{4,3,2,1,0:T(8,128)(2,1)S(1)}, bf16[4,4,4,152,128]{4,3,2,1,0:T(8,128)(2,1)}, u32[]{:S(2)}, u32[]{:S(2)}) collective-permute-start(bf16[4,4,4,152,128]{4,3,2,1,0:T(8,128)(2,1)S(1)} %pad_maximum_fusion.1.own_2), channel_id=1, source_target_pairs={{0,8},{8,0},{16,24},{24,16},{32,40},{40,32},{48,56},{56,48},{64,72... | collective-permute-start | bytes 7471112 | tf_op jit(solution)/shard_map/ppermute | solution.py:483
  95.3 4.9 collective-permute-done.11
  118.5 12.3 %shard_map.276 = (bf16[1088,1152]{1,0:T(8,128)(2,1)S(1)}, bf16[1088,2304]{1,0:T(8,128)(2,1)S(1)}, bf16[1088,1088]{1,0:T(8,128)(2,1)S(1)}) custom-call(s32[13]{0:T(128)S(1)} %copy-done.63, bf16[4,4,4,152,128]{4,3,2,1,0:T(8,128)(2,1)} %pad_maximum_fusion.own_1, bf16[4,4,4,152,128]{4,3,2,1,0:T(8,128)(2,1)} %collective-permute-done.13.sib_1, ...), custom_call_target="tpu_custom_call" | custom-call | bytes 31457280 | tf_op jit(solution)/shard_map/pallas_call | solution.py:757
  138.2 13.1 %shard_map.277 = (bf16[1088,4352]{1,0:T(8,128)(2,1)S(1)}, bf16[4352,1088]{1,0:T(8,128)(2,1)S(1)}) custom-call(bf16[2,2,4,4,2,912,128]{6,5,4,3,2,1,0:T(8,128)(2,1)} %bitcast.313, bf16[2,2,4,4,2,912,128]{6,5,4,3,2,1,0:T(8,128)(2,1)} %bitcast.314), custom_call_target="tpu_custom_call" | custom-call | bytes 41943040 | tf_op jit(solution)/shard_map/pallas_call | solution.py:709
  162.5 9.7 %shard_map.278 = (bf16[1088,1152]{1,0:T(8,128)(2,1)S(1)}, bf16[1088,2304]{1,0:T(8,128)(2,1)S(1)}, bf16[1088,1088]{1,0:T(8,128)(2,1)S(1)}) custom-call(bf16[2,2,4,4,2,912,128]{6,5,4,3,2,1,0:T(8,128)(2,1)} %bitcast.315), custom_call_target="tpu_custom_call" | custom-call | bytes 20971520 | tf_op jit(solution)/shard_map/pallas_call | solution.py:709
  184.8 8.1 %shard_map.279 = (bf16[128,1152]{1,0:T(8,128)(2,1)S(1)}, bf16[128,1152]{1,0:T(8,128)(2,1)S(1)}) custom-call(bf16[128,1152]{1,0:T(8,128)(2,1)S(1)} %fusion.5.q_ref, bf16[4,2,64,2304]{3,2,1,0:T(8,128)(2,1)} %pad_maximum_fusion.2.kv_own, bf16[4,2,64,2304]{3,2,1,0:T(8,128)(2,1)} %collective-permute-done.24.kv_sib, s32[128,1]{1,0:T(8,128)S(1)} %copy.151.lpos, ...), custom_call_target="tpu_custom_call" | custom-call | flops 8000000000 | bytes 6291456 | tf_op jit(solution)/shard_map/pallas_call | solution.py:231
  197.4 4.7 copy-done.67
  202.1 5.6 %shard_map.280 = (f32[128,1088]{1,0:T(8,128)S(1)}, bf16[128,1088]{1,0:T(8,128)(2,1)S(1)}, bf16[128,16]{1,0:T(8,128)(2,1)S(1)}, bf16[128,16]{1,0:T(8,128)(2,1)S(1...) custom-call(bf16[128,1152]{1,0:T(8,128)(2,1)S(1)} %get-tuple-element.219.ctx, ...), custom_call_target="tpu_custom_call" | custom-call | flops 10000000000 | bytes 25165824 | tf_op jit(solution)/shard_map/pallas_call | solution.py:425
  214.8 11.5 %all-gather.10.cloned.1.call-done = bf16[1,77824,128]{2,1,0:T(8,128)(2,1)} async-done(((bf16[1,608,128]{2,1,0:T(8,128)(2,1)}), bf16[1,77824,128]{2,1,0:T(8,128)(2,1)}) %all-gather.10.cloned.1.call-update) | async-done | bytes 19922960 | tf_op jit(solution)/shard_map/all_gather | solution.py:801
  226.3 5.7 %collective-permute-done.27 = bf16[2,64,2304]{2,1,0:T(8,128)(2,1)} collective-permute-done((bf16[2,64,2304]{2,1,0:T(8,128)(2,1)S(1)}, bf16[2,64,2304]{2,1,0:T(8,128)(2,1)}, u32[]{:S(2)}, u32[]{:S(2)}) %collective-permute-start.27) | collective-permute-done | bytes 589856 | tf_op jit(solution)/shard_map/ppermute | solution.py:471
  236.9 13.1 %shard_map.281 = (bf16[1088,4352]{1,0:T(8,128)(2,1)S(1)}, bf16[4352,1088]{1,0:T(8,128)(2,1)S(1)}) custom-call(bf16[2,2,4,4,2,608,128]{6,5,4,3,2,1,0:T(8,128)(2,1)} %bitcast.317, bf16[2,2,4,4,2,608,128]{6,5,4,3,2,1,0:T(8,128)(2,1)} %bitcast.318), custom_call_target="tpu_custom_call" | custom-call | bytes 41943040 | tf_op jit(solution)/shard_map/pallas_call | solution.py:709
  257.1 5.8 %shard_map.282 = (bf16[128,1152]{1,0:T(8,128)(2,1)S(1)}, bf16[128,1152]{1,0:T(8,128)(2,1)S(1)}) custom-call(bf16[128,1152]{1,0:T(8,128)(2,1)S(1)} %copy-done.18, bf16[4,2,64,2304]{3,2,1,0:T(8,128)(2,1)S(1)} %pad_maximum_fusion.3.kv_own, bf16[4,2,64,2304]{3,2,1,0:T(8,128)(2,1)S(1)} %collective-permute-done.31.kv_sib, s32[128,1]{1,0:T(8,128)S(1)} %copy-done.38, ...), custom_call_target="tpu_custom_call" | custom-call | flops 8000000000 | bytes 6291456 | tf_op jit(solution)/shard_map/pallas_call | solution.py:231
  265.9 16.4 %shard_map.283 = (bf16[128,1088]{1,0:T(8,128)(2,1)S(1)}, f32[128,1088]{1,0:T(8,128)S(1)}, bf16[128,1152]{1,0:T(8,128)(2,1)S(1)}, bf16[16,1088]{1,0:T(8,128)(2,1)...) custom-call(bf16[128,1152]{1,0:T(8,128)(2,1)S(1)} %get-tuple-element, ...), custom_call_target="tpu_custom_call" | custom-call | flops 17999998976 | bytes 25165824 | tf_op jit(solution)/shard_map/pallas_call | solution.py:425
  296.7 7.1 %shard_map.284.gq = bf16[128,1152]{1,0:T(8,128)(2,1)S(1)} custom-call(bf16[128,1152]{1,0:T(8,128)(2,1)S(1)} %get-tuple-element.243.qe_ref, bf16[128,1152]{1,0:T(8,128)(2,1)S(1)} %get-tuple-element.274.ge_ref, bf16[4,2,64,2304]{3,2,1,0:T(8,128)(2,1)S(1)} %pad_maximum_fusion.3.kv_own, bf16[4,2,64,2304]{3,2,1,0:T(8,128)(2,1)S(1)} %collective-permute-done.31.kv_sib, ...), custom_call_target="tpu_custom_call" | custom-call | flops 8000000000 | bytes 6291456 | tf_op jit(solution)/shard_map/pallas_call | solution.py:231
  317.4 10.5 %shard_map.285 = (bf16[2,64,1152]{2,1,0:T(8,128)(2,1)S(1)}, bf16[2,64,1152]{2,1,0:T(8,128)(2,1)S(1)}) custom-call(bf16[2,64,2304]{2,1,0:T(8,128)(2,1)S(1)} %bitcast.284, bf16[4,2,64,1152]{3,2,1,0:T(8,128)(2,1)} %pad_maximum_fusion.6.q_own, bf16[4,2,64,1152]{3,2,1,0:T(8,128)(2,1)} %collective-permute-done.40.q_sib, ...), custom_call_target="tpu_custom_call" | custom-call | flops 8000000000 | bytes 6291456 | tf_op jit(solution)/shard_map/pallas_call | solution.py:231
  341.4 17.3 %shard_map.287 = (f32[128,1088]{1,0:T(8,128)}, bf16[128,1152]{1,0:T(8,128)(2,1)}, bf16[16,1088]{1,0:T(8,128)(2,1)}, bf16[16,1088]{1,0:T(8,128)(2,1)}, bf16[16,10...) custom-call(f32[128,1088]{1,0:T(8,128)} %copy-done.75, ...), custom_call_target="tpu_custom_call" | custom-call | flops 16000000000 | bytes 25165824 | tf_op jit(solution)/shard_map/pallas_call | solution.py:425
  363.2 9.6 %shard_map.288.gq = bf16[128,1152]{1,0:T(8,128)(2,1)S(1)} custom-call(bf16[128,1152]{1,0:T(8,128)(2,1)S(1)} %get-tuple-element.218.qe_ref, bf16[128,1152]{1,0:T(8,128)(2,1)S(1)} %copy-done.16, bf16[4,2,64,2304]{3,2,1,0:T(8,128)(2,1)} %pad_maximum_fusion.2.kv_own, bf16[4,2,64,2304]{3,2,1,0:T(8,128)(2,1)} %collective-permute-done.24.kv_sib, ...), custom_call_target="tpu_custom_call" | custom-call | flops 8000000000 | bytes 6291456 | tf_op jit(solution)/shard_map/pallas_call | solution.py:231
  388.7 10.9 %shard_map.289 = (bf16[2,64,1152]{2,1,0:T(8,128)(2,1)S(1)}, bf16[2,64,1152]{2,1,0:T(8,128)(2,1)S(1)}) custom-call(bf16[2,64,2304]{2,1,0:T(8,128)(2,1)S(1)} %bitcast.280, bf16[4,2,64,1152]{3,2,1,0:T(8,128)(2,1)S(1)} %copy-done.9, bf16[4,2,64,1152]{3,2,1,0:T(8,128)(2,1)} %collective-permute-done.50.q_sib, bf16[4,2,64,1152]{3,2,1,0:T(8,128)(2,1)} %pad_maximum_fusion.8.g_own, ...), custom_call_target="tpu_custom_call" | custom-call | flops 8000000000 | bytes 6291456 | tf_op jit(solution)/shard_map/pallas_call | solution.py:231
  405.6 5.4 %all-to-all-start = ((bf16[8,16,2304]{2,1,0:T(8,128)(2,1)}), bf16[8,16,2304]{2,1,0:T(8,128)(2,1)S(1)}, u32[]{:S(2)}, u32[]{:S(2)}) async-start(bf16[8,16,2304]{2,1,0:T(8,128)(2,1)} %maximum_bitcast_fusion.5), calls=%async_computation | async-start | bytes 1179648 | tf_op jit(solution)/shard_map/all_to_all | solution.py:932
  412.6 8.7 %all-to-all-done = bf16[8,16,2304]{2,1,0:T(8,128)(2,1)S(1)} async-done(((bf16[8,16,2304]{2,1,0:T(8,128)(2,1)}), bf16[8,16,2304]{2,1,0:T(8,128)(2,1)S(1)}, u32[]{:S(2)}, u32[]{:S(2)}) %all-to-all-start) | async-done | bytes 589856 | tf_op jit(solution)/shard_map/all_to_all | solution.py:932
  449.3 21.9 %collective-permute-done.61 = bf16[2,1152,128]{2,1,0:T(8,128)(2,1)S(1)} collective-permute-done((bf16[2,1152,128]{2,1,0:T(8,128)(2,1)S(1)}, bf16[2,1152,128]{2,1,0:T(8,128)(2,1)S(1)}, u32[]{:S(2)}, u32[]{:S(2)}) %collective-permute-start.61) | collective-permute-done | bytes 589856 | tf_op jit(solution)/shard_map/ppermute | solution.py:471
  478.4 5.1 %collective-permute-start.67 = (bf16[4,2,1152,128]{3,2,1,0:T(8,128)(2,1)S(1)}, bf16[4,2,1152,128]{3,2,1,0:T(8,128)(2,1)}, u32[]{:S(2)}, u32[]{:S(2)}) collective-permute-start(bf16[4,2,1152,128]{3,2,1,0:T(8,128)(2,1)S(1)} %pad_maximum_fusion.4), channel_id=1, source_target_pairs={{0,8},{8,0},{16,24},{24,16},{32,40},{40,32},{48,56},{56,48},{64,72... | collective-permute-start | bytes 7077896 | tf_op jit(solution)/shard_map/ppermute | solution.py:483
  489.7 5.9 %shard_map.294 = (f32[2,1088,128]{2,1,0:T(8,128)}, f32[2,1088,128]{2,1,0:T(8,128)}, f32[2,1088,128]{2,1,0:T(8,128)}, f32[2,4352,128]{2,1,0:T(8,128)}, f32[2,3264...) custom-call(s32[8]{0:T(128)S(1)} %copy-done.62, ...), custom_call_target="tpu_custom_call", output_to_operand_aliasing={{0}: (3, {}), {1}: (4, {}), {2}: (5, {}), {3}: (6, {}), {4}... | custom-call | bytes 14680064 | tf_op jit(solution)/shard_map/pallas_call | solution.py:583
  (610 shorter events, 258.5 us)
Async XLA Ops:
  7.2 131.0 %all-gather.8.cloned.1.call-start = ((), (), s32[]{:S(2)}) async-start(), calls=%async_computation.1 | async-start | bytes 30117888 | tf_op jit(solution)/shard_map/all_gather | solution.py:801
  15.1 211.2 %all-gather.10.cloned.1.call-start = ((), (), s32[]{:S(2)}) async-start(), calls=%async_computation.2 | async-start | bytes 20078592 | tf_op jit(solution)/shard_map/all_gather | solution.py:801
  15.9 409.8 %all-gather.12.cloned.1.call-start = ((), (), s32[]{:S(2)}) async-start(), calls=%async_computation.3 | async-start | bytes 2506752 | tf_op jit(solution)/shard_map/all_gather | solution.py:917
  40.5 36.9 %collective-permute-start.19 = (bf16[2,64,1088]{2,1,0:T(8,128)(2,1)}, bf16[2,64,1088]{2,1,0:T(8,128)(2,1)}, u32[]{:S(2)}, u32[]{:S(2)}) collective-permute-start(bf16[2,64,1088]{2,1,0:T(8,128)(2,1)} %pad_maximum_fusion.12), channel_id=1, source_target_pairs={{0,64},{8,72},{16,80},{24,88},{32,96},{40,104},{48,112},{56,120},{... | collective-permute-start | bytes 835592 | tf_op jit(solution)/shard_map/ppermute | solution.py:809
  46.5 32.6 %collective-permute-start.10 = (bf16[4,4,152,128]{3,2,1,0:T(8,128)(2,1)S(1)}, bf16[4,4,152,128]{3,2,1,0:T(8,128)(2,1)}, u32[]{:S(2)}, u32[]{:S(2)}) collective-permute-start(bf16[4,4,152,128]{3,2,1,0:T(8,128)(2,1)S(1)} %pad_maximum_fusion.9), channel_id=1, source_target_pairs={{0,65},{8,73},{2,67},{10,75},{4,69},{12,77},{6,71},{14,79},{16,81}... | collective-permute-start | bytes 1867784 | tf_op jit(solution)/shard_map/ppermute | solution.py:734
  47.7 35.3 %collective-permute-start.9 = (bf16[4,4,152,128]{3,2,1,0:T(8,128)(2,1)S(1)}, bf16[4,4,152,128]{3,2,1,0:T(8,128)(2,1)}, u32[]{:S(2)}, u32[]{:S(2)}) collective-permute-start(bf16[4,4,152,128]{3,2,1,0:T(8,128)(2,1)S(1)} %pad_maximum_fusion.9), channel_id=1, source_target_pairs={{0,1},{8,9},{2,3},{10,11},{4,5},{12,13},{6,7},{14,15},{16,17},{24,... | collective-permute-start | bytes 1867784 | tf_op jit(solution)/shard_map/ppermute | solution.py:733
  48.1 23.6 %collective-permute-start.15 = (bf16[4,4,152,128]{3,2,1,0:T(8,128)(2,1)S(1)}, bf16[4,4,152,128]{3,2,1,0:T(8,128)(2,1)}, u32[]{:S(2)}, u32[]{:S(2)}) collective-permute-start(bf16[4,4,152,128]{3,2,1,0:T(8,128)(2,1)S(1)} %pad_maximum_fusion.10), channel_id=1, source_target_pairs={{0,48},{8,56},{16,0},{24,8},{32,16},{40,24},{48,32},{56,40},{64,11... | collective-permute-start | bytes 1867784 | tf_op jit(solution)/shard_map/ppermute | solution.py:734
  50.4 25.9 %collective-permute-start.14 = (bf16[4,4,152,128]{3,2,1,0:T(8,128)(2,1)S(1)}, bf16[4,4,152,128]{3,2,1,0:T(8,128)(2,1)}, u32[]{:S(2)}, u32[]{:S(2)}) collective-permute-start(bf16[4,4,152,128]{3,2,1,0:T(8,128)(2,1)S(1)} %pad_maximum_fusion.10), channel_id=1, source_target_pairs={{0,16},{8,24},{16,32},{24,40},{32,48},{40,56},{48,0},{56,8},{64,80... | collective-permute-start | bytes 1867784 | tf_op jit(solution)/shard_map/ppermute | solution.py:733
  86.1 27.0 %collective-permute-start.18 = (bf16[4,4,4,152,128]{4,3,2,1,0:T(8,128)(2,1)S(1)}, bf16[4,4,4,152,128]{4,3,2,1,0:T(8,128)(2,1)}, u32[]{:S(2)}, u32[]{:S(2)}) collective-permute-start(bf16[4,4,4,152,128]{4,3,2,1,0:T(8,128)(2,1)S(1)} %pad_maximum_fusion.1.own_2), channel_id=1, source_target_pairs={{0,8},{8,0},{16,24},{24,16},{32,40},{40,32},{48,56},{56,48},{64,72... | collective-permute-start | bytes 7471112 | tf_op jit(solution)/shard_map/ppermute | solution.py:483
  134.4 24.3 %collective-permute-start.20 = (bf16[2,64,2304]{2,1,0:T(8,128)(2,1)S(1)}, bf16[2,64,2304]{2,1,0:T(8,128)(2,1)S(1)}, u32[]{:S(2)}, u32[]{:S(2)}) collective-permute-start(bf16[2,64,2304]{2,1,0:T(8,128)(2,1)S(1)} %bitcast.277), channel_id=1, source_target_pairs={{0,16},{8,24},{16,32},{24,40},{32,48},{40,56},{48,0},{56,8},{64,80... | collective-permute-start | bytes 1769480 | tf_op jit(solution)/shard_map/ppermute | solution.py:471
  134.4 24.3 %collective-permute-start.21 = (bf16[2,64,2304]{2,1,0:T(8,128)(2,1)S(1)}, bf16[2,64,2304]{2,1,0:T(8,128)(2,1)}, u32[]{:S(2)}, u32[]{:S(2)}) collective-permute-start(bf16[2,64,2304]{2,1,0:T(8,128)(2,1)S(1)} %bitcast.278), channel_id=1, source_target_pairs={{0,48},{8,56},{16,0},{24,8},{32,16},{40,24},{48,32},{56,40},{64,11... | collective-permute-start | bytes 1769480 | tf_op jit(solution)/shard_map/ppermute | solution.py:471
  210.5 21.5 %collective-permute-start.27 = (bf16[2,64,2304]{2,1,0:T(8,128)(2,1)S(1)}, bf16[2,64,2304]{2,1,0:T(8,128)(2,1)}, u32[]{:S(2)}, u32[]{:S(2)}) collective-permute-start(bf16[2,64,2304]{2,1,0:T(8,128)(2,1)S(1)} %bitcast.281), channel_id=1, source_target_pairs={{0,16},{8,24},{16,32},{24,40},{32,48},{40,56},{48,0},{56,8},{64,80... | collective-permute-start | bytes 1769480 | tf_op jit(solution)/shard_map/ppermute | solution.py:471
  210.6 21.4 %collective-permute-start.28 = (bf16[2,64,2304]{2,1,0:T(8,128)(2,1)S(1)}, bf16[2,64,2304]{2,1,0:T(8,128)(2,1)}, u32[]{:S(2)}, u32[]{:S(2)}) collective-permute-start(bf16[2,64,2304]{2,1,0:T(8,128)(2,1)S(1)} %bitcast.282), channel_id=1, source_target_pairs={{0,48},{8,56},{16,0},{24,8},{32,16},{40,24},{48,32},{56,40},{64,11... | collective-permute-start | bytes 1769480 | tf_op jit(solution)/shard_map/ppermute | solution.py:471
  253.0 29.4 %collective-permute-start.25 = (bf16[2,64,1152]{2,1,0:T(8,128)(2,1)S(1)}, bf16[2,64,1152]{2,1,0:T(8,128)(2,1)S(1)}, u32[]{:S(2)}, u32[]{:S(2)}) collective-permute-start(bf16[2,64,1152]{2,1,0:T(8,128)(2,1)S(1)} %bitcast.292), channel_id=1, source_target_pairs={{0,16},{8,24},{16,32},{24,40},{32,48},{40,56},{48,0},{56,8},{64,80... | collective-permute-start | bytes 884744 | tf_op jit(solution)/shard_map/ppermute | solution.py:471
  253.1 29.4 %collective-permute-start.26 = (bf16[2,64,1152]{2,1,0:T(8,128)(2,1)S(1)}, bf16[2,64,1152]{2,1,0:T(8,128)(2,1)S(1)}, u32[]{:S(2)}, u32[]{:S(2)}) collective-permute-start(bf16[2,64,1152]{2,1,0:T(8,128)(2,1)S(1)} %bitcast.293), channel_id=1, source_target_pairs={{0,48},{8,56},{16,0},{24,8},{32,16},{40,24},{48,32},{56,40},{64,11... | collective-permute-start | bytes 884744 | tf_op jit(solution)/shard_map/ppermute | solution.py:471
  262.9 19.6 %collective-permute-start.32 = (bf16[2,64,1152]{2,1,0:T(8,128)(2,1)S(1)}, bf16[2,64,1152]{2,1,0:T(8,128)(2,1)S(1)}, u32[]{:S(2)}, u32[]{:S(2)}) collective-permute-start(bf16[2,64,1152]{2,1,0:T(8,128)(2,1)S(1)} %bitcast.298), channel_id=1, source_target_pairs={{0,16},{8,24},{16,32},{24,40},{32,48},{40,56},{48,0},{56,8},{64,80... | collective-permute-start | bytes 884744 | tf_op jit(solution)/shard_map/ppermute | solution.py:471
  337.3 24.2 %collective-permute-start.47 = (bf16[16,2304]{1,0:T(8,128)(2,1)S(1)}, bf16[16,2304]{1,0:T(8,128)(2,1)S(1)}, u32[]{:S(2)}, u32[]{:S(2)}) collective-permute-start(bf16[16,2304]{1,0:T(8,128)(2,1)S(1)} %get-tuple-element.373), channel_id=1, source_target_pairs={{0,32},{8,40},{16,48},{24,56},{32,0},{40,8},{48,16},{56,24},{64,96... | collective-permute-start | bytes 221192 | tf_op jit(solution)/shard_map/ppermute | solution.py:497
  339.4 22.0 %collective-permute-start.46 = (bf16[16,2304]{1,0:T(8,128)(2,1)S(1)}, bf16[16,2304]{1,0:T(8,128)(2,1)S(1)}, u32[]{:S(2)}, u32[]{:S(2)}) collective-permute-start(bf16[16,2304]{1,0:T(8,128)(2,1)S(1)} %get-tuple-element.374), channel_id=1, source_target_pairs={{0,48},{8,56},{16,0},{24,8},{32,16},{40,24},{48,32},{56,40},{64,11... | collective-permute-start | bytes 221192 | tf_op jit(solution)/shard_map/ppermute | solution.py:497
  340.5 21.0 %collective-permute-start.45 = (bf16[16,2304]{1,0:T(8,128)(2,1)S(1)}, bf16[16,2304]{1,0:T(8,128)(2,1)S(1)}, u32[]{:S(2)}, u32[]{:S(2)}) collective-permute-start(bf16[16,2304]{1,0:T(8,128)(2,1)S(1)} %get-tuple-element.372), channel_id=1, source_target_pairs={{0,16},{8,24},{16,32},{24,40},{32,48},{40,56},{48,0},{56,8},{64,80... | collective-permute-start | bytes 221192 | tf_op jit(solution)/shard_map/ppermute | solution.py:497
  411.1 72.4 %all-gather.14.cloned.1.call-start = ((), (), s32[]{:S(2)}) async-start(), calls=%async_computation.4 | async-start | bytes 5308416 | tf_op jit(solution)/shard_map/all_gather | solution.py:938
  443.3 27.8 %collective-permute-start.61 = (bf16[2,1152,128]{2,1,0:T(8,128)(2,1)S(1)}, bf16[2,1152,128]{2,1,0:T(8,128)(2,1)S(1)}, u32[]{:S(2)}, u32[]{:S(2)}) collective-permute-start(bf16[2,1152,128]{2,1,0:T(8,128)(2,1)S(1)} %bitcast.285), channel_id=1, source_target_pairs={{0,16},{8,24},{16,32},{24,40},{32,48},{40,56},{48,0},{56,8},{64,80... | collective-permute-start | bytes 1769480 | tf_op jit(solution)/shard_map/ppermute | solution.py:471
  443.7 30.3 %collective-permute-start.66 = (bf16[64,1088]{1,0:T(8,128)(2,1)S(1)}, bf16[64,1088]{1,0:T(8,128)(2,1)S(1)}, u32[]{:S(2)}, u32[]{:S(2)}) collective-permute-start(bf16[64,1088]{1,0:T(8,128)(2,1)S(1)} %get-tuple-element.392), channel_id=1, source_target_pairs={{0,64},{8,72},{16,80},{24,88},{32,96},{40,104},{48,112},{56,120},{... | collective-permute-start | bytes 417800 | tf_op jit(solution)/shard_map/ppermute | solution.py:943
  445.1 26.3 %collective-permute-start.62 = (bf16[2,1152,128]{2,1,0:T(8,128)(2,1)S(1)}, bf16[2,1152,128]{2,1,0:T(8,128)(2,1)S(1)}, u32[]{:S(2)}, u32[]{:S(2)}) collective-permute-start(bf16[2,1152,128]{2,1,0:T(8,128)(2,1)S(1)} %bitcast.286), channel_id=1, source_target_pairs={{0,48},{8,56},{16,0},{24,8},{32,16},{40,24},{48,32},{56,40},{64,11... | collective-permute-start | bytes 1769480 | tf_op jit(solution)/shard_map/ppermute | solution.py:471
  447.5 27.3 %collective-permute-start.65 = (f32[64,1088]{1,0:T(8,128)S(1)}, f32[64,1088]{1,0:T(8,128)S(1)}, u32[]{:S(2)}, u32[]{:S(2)}) collective-permute-start(f32[64,1088]{1,0:T(8,128)S(1)} %get-tuple-element.371), channel_id=1, source_target_pairs={{0,64},{8,72},{16,80},{24,88},{32,96},{40,104},{48,112},{56,120},{... | collective-permute-start | bytes 835592 | tf_op jit(solution)/shard_map/ppermute | solution.py:943
  (179 other events, 1787.1 us)
Sparse Core Ops, SparseCore 0:
  15.2 120.4 all-gather.7
  138.7 87.5 all-gather.9
  380.0 43.0 all-gather.11
  429.4 46.5 all-gather.13
